TPU v7x, 32 devices: a whole 2x2x4 slice. The times are simulated.
32 devices in a mesh: group: 16 (over z, y, core), tp: 2 (over x).
Axes of the slice: x: 2, y: 2, z: 4, core: 2. Of those that a mesh axis runs over, the one named last changes fastest.
Arguments:
- queries: bfloat16 [1024, 2048], P('group', 'tp'), may hold values from -22 to 22
- new_kv: bfloat16 [1024, 1024], P('group', 'tp'), may hold values from -6 to 6
- local_cache: bfloat16 [4096, 1024], P('group', 'tp'), may hold values from -6 to 6
- remote_pool: bfloat16 [2048, 1024], P('group', 'tp'), may hold values from -6 to 6
- page_index: int32 [16, 16], P('group'), may hold values from 0 to 15, each once within a row
- lengths: int32 [16], P('group'), may hold values from 256 to 384, as said below
- sinks: float32 [32], P('tp'), may hold values from 4 to 8
- out_weight: bfloat16 [2048, 2880], P('tp'), may hold values from -0.125 to 0.125
- residual: bfloat16 [1024, 2880], P('group', 'tp'), may hold values from -6 to 6
- norm_gain: float32 [2880], replicated, may hold values from 0.5 to 2
- routes: int32 [1024, 4], P('group'), may hold values from 0 to 7, all different within a row; in each aligned block of 64 rows (0 to 63, 64 to 127, ...) at most 40 rows name the same one
- route_weights: float32 [1024, 4], P('group'), may hold values from 0.1 to 1
- expert_gate: bfloat16 [16, 2880, 1440], P('group', None, 'tp'), may hold values from -0.109375 to 0.109375
- expert_up: bfloat16 [16, 2880, 1440], P('group', None, 'tp'), may hold values from -0.109375 to 0.109375
- expert_down: bfloat16 [16, 1440, 2880], P('group', None, 'tp'), may hold values from -0.109375 to 0.109375
Outputs:
- layer_out: bfloat16 [1024, 2880], P('group', 'tp')
Inputs may be any that keep to these rules, and one draw needn't show every extreme that they name: `lengths`: every request has at least 256 cached positions; some request has exactly 256, some exactly 384. `routes`: within the rows of one request no expert is named by more than 40 rows. `page_index`: each row is a permutation.
All inputs are finite; a program needn't handle non-finite values.
Results may differ from a plain program's by a relative error of at most 0.013.
Values may be sent and summed in bfloat16 or wider, within the bound.
No kernel may reach another device: no remote copies, remote signals or barrier semaphores. Data moves between devices by JAX's collectives and lax.ppermute only.
A program may use at most 128 MiB of HBM per device.

v0:
```python
import functools

import jax
import jax.numpy as jnp
from jax import lax
from jax.experimental import pallas as pl
from jax.experimental.pallas import tpu as pltpu
from jax.sharding import PartitionSpec as P

HEAD = 64
TILE = 256
PARTS = 1
VMEM_LIMIT = 24 * 1024 * 1024


THETA = 150000.0
ALPHA = 1.702
EPSILON = 1e-05


def exchange(value, axis, offset):
    if offset == 0:
        return value
    size = lax.axis_size(axis)
    return lax.ppermute(value, axis, [(i, i ^ offset) for i in range(size)])


NT = (((1,), (1,)), ((), ()))


def dot_nt(left, right):
    return lax.dot_general(left, right, NT, preferred_element_type=jnp.float32)


def swapped_halves(value):
    lanes = value.shape[1]
    lane = lax.broadcasted_iota(jnp.int32, value.shape, 1)
    return jnp.where(
        lane % HEAD < HEAD // 2,
        pltpu.roll(value, lanes - HEAD // 2, 1),
        pltpu.roll(value, HEAD // 2, 1),
    )


def local_kernel(sink_ref, query_ref, kv_ref, local_ref, cos_ref, sin_ref, rotated_ref, state_ref):
    tokens = query_ref.shape[0]
    pair = 2 * HEAD
    kv_heads = kv_ref.shape[1] // pair
    group_size = query_ref.shape[1] // HEAD // kv_heads
    rows = group_size * tokens
    cosine, sine = cos_ref[...], sin_ref[...]
    low = lax.broadcasted_iota(jnp.int32, (tokens, pair), 1) < HEAD
    lane = lax.broadcasted_iota(jnp.int32, (rows, pair), 1)

    def rotated(value):
        return value * cosine + swapped_halves(value) * sine

    token_row = lax.broadcasted_iota(jnp.int32, (rows, tokens), 0) % tokens
    causal = lax.broadcasted_iota(jnp.int32, (rows, tokens), 1) <= token_row
    for h in range(kv_heads):
        lanes = slice(h * pair, (h + 1) * pair)
        own = kv_ref[:, lanes]
        own = jnp.where(low, rotated(own.astype(jnp.float32)).astype(jnp.bfloat16), own)
        queries = []
        for i in range(group_size // 2):
            start = (h * group_size + 2 * i) * HEAD
            both = rotated(query_ref[:, start : start + pair].astype(jnp.float32)) * HEAD**-0.5
            queries.append(jnp.where(low, both, 0.0))
            queries.append(jnp.where(low, pltpu.roll(both, HEAD, 1), 0.0))
        query = jnp.concatenate(queries, axis=0).astype(jnp.bfloat16)
        sink = jnp.concatenate(
            [jnp.full((tokens, 1), sink_ref[h * group_size + i]) for i in range(group_size)], axis=0
        )
        sources = [local_ref[:, lanes], own]
        scores = [dot_nt(query, source) for source in sources]
        scores[1] = jnp.where(causal, scores[1], -jnp.inf)
        row_max = sink
        for score in scores:
            row_max = jnp.maximum(row_max, jnp.max(score, axis=1, keepdims=True))
        denominator = jnp.exp(sink - row_max)
        blended = None
        for score, source in zip(scores, sources):
            weights = jnp.exp(score - row_max)
            denominator = denominator + jnp.sum(weights, axis=1, keepdims=True)
            term = jnp.dot(weights.astype(jnp.bfloat16), source, preferred_element_type=jnp.float32)
            blended = term if blended is None else blended + term
        place = slice(h * rows, (h + 1) * rows)
        rotated_ref[place, :] = query
        state_ref[place, :] = jnp.where(lane == 0, row_max, jnp.where(lane == 1, denominator, blended))


def split_copies(source, target, sems, first, parts):
    rows = source.shape[0]
    step = rows if parts == 1 else -(-rows // parts) // 16 * 16 + 16
    return [
        pltpu.make_async_copy(
            source.at[start : min(start + step, rows)],
            target.at[start : min(start + step, rows)],
            sems.at[first + i],
        )
        for i, start in enumerate(range(0, rows, step))
    ]


def start_all(copies):
    for copy in copies:
        copy.start()


def wait_all(copies):
    for copy in copies:
        copy.wait()


def page_kernel(me_ref, weight_ref, rotated_ref, state_ref, page_ref, valid_ref, attended_ref, *refs):
    other_refs, held_ref, sems = refs[:-2], refs[-2], refs[-1]
    copies = [
        split_copies(weight_ref.at[me_ref[0] ^ (j + 1)], held_ref.at[j], sems, 2 * j, 2)
        for j in range(len(other_refs))
    ]
    for some in copies:
        start_all(some)
    tokens = attended_ref.shape[0]
    pair = 2 * HEAD
    kv_heads = page_ref.shape[1] // pair
    rows = rotated_ref.shape[0] // kv_heads
    group_size = rows // tokens
    low = lax.broadcasted_iota(jnp.int32, (tokens, pair), 1) < HEAD
    page_valid = valid_ref[...] > 0.0
    for h in range(kv_heads):
        place = slice(h * rows, (h + 1) * rows)
        source = page_ref[:, h * pair : (h + 1) * pair]
        state = state_ref[place, :]
        score = jnp.where(page_valid, dot_nt(rotated_ref[place, :], source), -jnp.inf)
        row_max = jnp.maximum(state[:, 0:1], jnp.max(score, axis=1, keepdims=True))
        weights = jnp.exp(score - row_max)
        kept = jnp.exp(state[:, 0:1] - row_max)
        denominator = state[:, 1:2] * kept + jnp.sum(weights, axis=1, keepdims=True)
        term = jnp.dot(weights.astype(jnp.bfloat16), source, preferred_element_type=jnp.float32)
        blended = (state * kept + term) / denominator
        for i in range(group_size // 2):
            even = blended[2 * i * tokens : (2 * i + 1) * tokens]
            odd = blended[(2 * i + 1) * tokens : (2 * i + 2) * tokens]
            start = (h * group_size + 2 * i) * HEAD
            attended_ref[:, start : start + pair] = jnp.where(
                low, pltpu.roll(even, HEAD, 1), odd
            ).astype(jnp.bfloat16)
    attended = attended_ref[...]
    for j, ref in enumerate(other_refs):
        wait_all(copies[j])
        ref[...] = dot_nt(attended, held_ref[j]).astype(jnp.bfloat16)


def own_columns_kernel(
    me_ref, weight_ref, residual_ref, attended_ref, out_ref, sent_ref, held_ref, rows_ref, sems
):
    copies = split_copies(weight_ref.at[me_ref[0]], held_ref, sems, 0, PARTS)
    copies.append(pltpu.make_async_copy(residual_ref, rows_ref, sems.at[PARTS]))
    start_all(copies)
    wait_all(copies)
    terms = rows_ref[...].astype(jnp.float32) + dot_nt(attended_ref[...], held_ref[...])
    out_ref[...] = terms
    sent_ref[...] = terms.astype(jnp.bfloat16)


def tiles(size):
    return [slice(start, min(start + TILE, size)) for start in range(0, size, TILE)]


def gate_up_kernel(parts, me_ref, gate_ref, up_ref, gain_ref, *refs):
    sets, (out_ref, place_ref, row_ref, gate_held, up_held, gain_held, sems) = refs[:-7], refs[-7:]
    rows, width = sets[0].shape[1:]
    features, hidden = gate_ref.shape[1], gate_ref.shape[0]
    gain_copy = pltpu.make_async_copy(gain_ref, gain_held, sems.at[0])
    gain_copy.start()
    copies = []
    for t, tile in enumerate(tiles(hidden)):
        some = split_copies(gate_ref.at[tile], gate_held.at[tile], sems, 1 + 4 * t, 2)
        some += split_copies(up_ref.at[tile], up_held.at[tile], sems, 3 + 4 * t, 2)
        start_all(some)
        copies.append(some)
    me = me_ref[0]
    gain_copy.wait()
    for s, ref in enumerate(sets):
        held = [ref[j].astype(jnp.float32) for j in range(parts)]
        square = sum(jnp.sum(h * h, axis=1, keepdims=True) for h in held)
        scale = lax.rsqrt(square / features + EPSILON)
        for j in range(parts):
            place_ref[me ^ j] = held[j] * scale
        whole = jnp.concatenate([place_ref[p] for p in range(parts)], axis=1)
        row_ref[pl.ds(s * rows, rows), :] = (whole * gain_held[...]).astype(jnp.bfloat16)
    for t, tile in enumerate(tiles(hidden)):
        wait_all(copies[t])
        gate_val = dot_nt(row_ref[...], gate_held[tile])
        up_val = dot_nt(row_ref[...], up_held[tile])
        active = gate_val * jax.nn.sigmoid(ALPHA * gate_val) * (up_val + 1.0)
        out_ref[:, tile] = active.astype(jnp.bfloat16)


def down_kernel(me_ref, down_ref, *refs):
    own_ref, other_ref, held_ref, total_ref, sems = refs[-5:]
    actives = refs[:-5]
    rows, width = own_ref.shape
    copies = [
        split_copies(down_ref.at[me_ref[0] ^ j], held_ref.at[j], sems, PARTS * j, PARTS)
        for j in range(len(actives))
    ]
    for some in copies:
        start_all(some)
    for j, ref in enumerate(actives):
        wait_all(copies[j])
        for tile in tiles(width):
            term = jnp.dot(ref[...], held_ref[j, :, tile], preferred_element_type=jnp.float32)
            if j > 0:
                term = term + total_ref[:, tile]
            if j < len(actives) - 1:
                total_ref[:, tile] = term
            else:
                own_ref[:, tile] = term[:rows].astype(jnp.bfloat16)
                other_ref[:, tile] = term[rows:].astype(jnp.bfloat16)


def kernel_call(kernel, out_types, scalars, sources, *operands, scratch=()):
    in_vmem = pl.BlockSpec(memory_space=pltpu.VMEM)
    in_hbm = pl.BlockSpec(memory_space=pltpu.HBM)
    return pl.pallas_call(
        kernel,
        out_shape=[pltpu.VMEM(shape, dtype) for shape, dtype in out_types],
        in_specs=[pl.BlockSpec(memory_space=pltpu.SMEM)] * len(scalars)
        + [in_hbm] * len(sources)
        + [in_vmem] * len(operands),
        out_specs=[in_vmem] * len(out_types),
        scratch_shapes=scratch,
        compiler_params=pltpu.CompilerParams(vmem_limit_bytes=VMEM_LIMIT),
    )(
        *scalars,
        *[pltpu.with_memory_space_constraint(value, pltpu.HBM) for value in sources],
        *[pltpu.with_memory_space_constraint(value, pltpu.VMEM) for value in operands],
    )


def on_device(
    queries,
    new_kv,
    local_cache,
    remote_pool,
    page_index,
    lengths,
    sinks,
    out_weight,
    residual,
    norm_gain,
    routes,
    route_weights,
    expert_gate,
    expert_up,
    expert_down,
):
    groups = lax.axis_size("group")
    tp = lax.axis_size("tp")
    me_tp = lax.axis_index("tp")
    experts = groups // 2
    me_expert = lax.axis_index("group") // 2
    tp_scalar = me_tp.astype(jnp.int32).reshape(1)
    lane_count = remote_pool.shape[1]
    local_len = local_cache.shape[0]
    fetched = lax.all_to_all(
        remote_pool.reshape(groups, -1, lane_count),
        "group",
        split_axis=0,
        concat_axis=0,
        tiled=True,
    )
    page_len = fetched.shape[1]
    length = lengths[0]
    offsets = jnp.arange(page_len, dtype=jnp.int32)
    remote_pos = local_len + page_index[0][:, None] * page_len + offsets[None, :]
    page_valid = (remote_pos < length).astype(jnp.float32).reshape(1, -1)
    block_len, width = residual.shape
    positions = (length + jnp.arange(block_len, dtype=jnp.int32)).astype(jnp.float32)
    lane = jnp.arange(2 * HEAD, dtype=jnp.int32) % HEAD
    inverse = THETA ** (-2.0 * (lane % (HEAD // 2)).astype(jnp.float32) / HEAD)
    angles = positions[:, None] * inverse[None, :]
    sine = jnp.where(lane < HEAD // 2, -1.0, 1.0)[None, :] * jnp.sin(angles)
    hidden = expert_gate.shape[2]
    weight = out_weight.T.reshape(tp, width, out_weight.shape[0])
    gate, up = expert_gate[0].T, expert_up[0].T
    down = expert_down.reshape(tp, hidden, width)
    dma = pltpu.SemaphoreType.DMA
    in_vmem = pl.BlockSpec(memory_space=pltpu.VMEM)
    states = block_len * queries.shape[1] // HEAD
    rotated, state = pl.pallas_call(
        local_kernel,
        out_shape=[
            pltpu.VMEM((states, 2 * HEAD), jnp.bfloat16),
            pltpu.VMEM((states, 2 * HEAD), jnp.float32),
        ],
        in_specs=[pl.BlockSpec(memory_space=pltpu.SMEM)] + [in_vmem] * 5,
        out_specs=[in_vmem] * 2,
        compiler_params=pltpu.CompilerParams(vmem_limit_bytes=VMEM_LIMIT),
    )(
        sinks,
        *[pltpu.with_memory_space_constraint(value, pltpu.HBM) for value in (queries, new_kv, local_cache)],
        *[pltpu.with_memory_space_constraint(value, pltpu.VMEM) for value in (jnp.cos(angles), sine)],
    )
    attended, *others = kernel_call(
        page_kernel,
        [(queries.shape, jnp.bfloat16)] + [(residual.shape, jnp.bfloat16)] * (tp - 1),
        [tp_scalar],
        [weight],
        rotated,
        state,
        fetched.reshape(-1, lane_count),
        page_valid,
        scratch=[pltpu.VMEM((tp - 1, *weight.shape[1:]), jnp.bfloat16), dma((2 * (tp - 1),))],
    )
    arriving = [exchange(other, "tp", j + 1) for j, other in enumerate(others)]
    gain, route_weights, _ = lax.optimization_barrier((norm_gain, route_weights, attended))
    gain = gain.reshape(1, tp * width)
    own_state, own_terms = kernel_call(
        own_columns_kernel,
        [(residual.shape, jnp.float32), (residual.shape, jnp.bfloat16)],
        [tp_scalar],
        [weight, residual],
        lax.optimization_barrier((attended, gain))[0],
        scratch=[
            pltpu.VMEM(weight.shape[1:], jnp.bfloat16),
            pltpu.VMEM(residual.shape, jnp.bfloat16),
            dma((PARTS + 1,)),
        ],
    )
    for term in arriving:
        own_state = own_state + term.astype(jnp.float32)
    state_sent = own_state.astype(jnp.bfloat16)
    if tp == 2:
        own_terms = lax.optimization_barrier((own_terms, state_sent))[0]
        other_state = exchange(own_terms, "tp", 1).astype(jnp.float32) + others[0].astype(jnp.float32)
        own_blocks = [state_sent, other_state.astype(jnp.bfloat16)]
    else:
        own_blocks = [exchange(state_sent, "tp", j) for j in range(tp)]

    top_count = routes.shape[1]
    capacity = 5 * block_len * top_count // (4 * experts)
    half = experts // 2
    mixing = route_weights / jnp.sum(route_weights, axis=1, keepdims=True)
    plan = jnp.concatenate([routes.astype(jnp.float32), mixing], axis=1)
    far_plan = exchange(lax.optimization_barrier((plan, own_blocks[-1]))[0], "group", experts)

    def slots(chosen_experts, weights):
        chosen = (chosen_experts ^ me_expert)[:, :, None] == jnp.arange(half, dtype=jnp.int32)
        member = jnp.any(chosen, axis=1)
        mix = jnp.sum(jnp.where(chosen, weights[:, :, None], 0.0), axis=1)
        earlier = jnp.arange(block_len)[:, None] > jnp.arange(block_len)[None, :]
        rank = jnp.dot(
            earlier.astype(jnp.bfloat16), member.astype(jnp.bfloat16), preferred_element_type=jnp.float32
        ).astype(jnp.int32)
        hit = member.T[:, None, :] & (
            rank.T[:, None, :] == jnp.arange(capacity, dtype=jnp.int32)[None, :, None]
        )
        pick = hit.astype(jnp.bfloat16).reshape(half * capacity, block_len)
        spread = jnp.where(hit, mix.T[:, None, :], 0.0).reshape(half * capacity, block_len)
        high = spread.astype(jnp.bfloat16)
        return pick, (high, (spread - high.astype(jnp.float32)).astype(jnp.bfloat16))

    own_pick, own_spread = slots(routes, mixing)

    def after(value, *earlier):
        return lax.optimization_barrier((value, *earlier))[0]

    def whole(value):
        return [exchange(value, "tp", j) for j in range(tp)]

    def picked(pick, values):
        parts = [
            jnp.dot(pick, value, preferred_element_type=jnp.float32)
            .astype(jnp.bfloat16)
            .reshape(half, capacity, width)
            for value in values
        ]
        return jnp.stack(parts, axis=1)

    def send_rows(rows):
        return [exchange(rows[d], "group", 2 * d) for d in range(half)]

    def blend(spread, pieces):
        rows = jnp.concatenate(pieces, axis=0)
        rows_first = (((0,), (0,)), ((), ()))
        return sum(
            lax.dot_general(part, rows, rows_first, preferred_element_type=jnp.float32)
            for part in spread
        )

    def activate(sets):
        rows = sets[0].shape[1]
        (active,) = kernel_call(
            functools.partial(gate_up_kernel, tp),
            [((2 * rows, hidden), jnp.bfloat16)],
            [tp_scalar],
            [gate, up, gain],
            *sets,
            scratch=[
                pltpu.VMEM((tp, rows, width), jnp.float32),
                pltpu.VMEM((2 * rows, tp * width), jnp.bfloat16),
                pltpu.VMEM(gate.shape, jnp.bfloat16),
                pltpu.VMEM(up.shape, jnp.bfloat16),
                pltpu.VMEM(gain.shape, jnp.float32),
                dma((1 + 4 * len(tiles(hidden)),)),
            ],
        )
        return active

    def project_down(actives):
        rows = actives[0].shape[0] // 2
        return kernel_call(
            down_kernel,
            [((rows, width), jnp.bfloat16)] * 2,
            [tp_scalar],
            [down],
            *actives,
            scratch=[
                pltpu.VMEM(down.shape, jnp.bfloat16),
                pltpu.VMEM((2 * rows, width), jnp.float32),
                dma((PARTS * tp,)),
            ],
        )

    def add_halves(mine, theirs):
        summed = mine.astype(jnp.float32) + exchange(theirs, "group", 1).astype(jnp.float32)
        return summed.astype(jnp.bfloat16).reshape(half, capacity, width)

    far_blocks = whole(exchange(state_sent, "group", experts))
    own_sent = picked(own_pick, own_blocks)
    own_pieces = send_rows(own_sent)
    far_plan = after(far_plan, own_pieces[1])
    far_pick, far_spread = slots(
        far_plan[:, :top_count].astype(jnp.int32), far_plan[:, top_count:]
    )
    far_sent = picked(far_pick, far_blocks)
    far_pieces = send_rows(far_sent)
    own_rows = jnp.concatenate([after(piece, far_sent) for piece in own_pieces], axis=1)
    own_active = activate([own_rows, exchange(own_rows, "group", 1)])
    own_actives = whole(own_active)
    far_rows = jnp.concatenate([after(piece, own_active) for piece in far_pieces], axis=1)
    far_active = activate([far_rows, exchange(far_rows, "group", 1)])
    far_actives = whole(far_active)
    own_actives[0] = after(own_actives[0], far_active)
    own_out = project_down(own_actives)
    far_actives[0] = after(far_actives[0], own_out[0])
    far_out = add_halves(*project_down(far_actives))
    own_out = add_halves(*own_out)
    far_sum = blend(far_spread, send_rows(far_out)).astype(jnp.bfloat16)
    far_sum = exchange(far_sum, "group", experts)
    total = own_state + blend(own_spread, send_rows(own_out)) + far_sum.astype(jnp.float32)
    return total.astype(jnp.bfloat16)


def solution(mesh):
    return jax.shard_map(
        on_device,
        mesh=mesh,
        in_specs=(
            P("group", "tp"),
            P("group", "tp"),
            P("group", "tp"),
            P("group", "tp"),
            P("group", None),
            P("group"),
            P("tp"),
            P("tp", None),
            P("group", "tp"),
            P(),
            P("group", None),
            P("group", None),
            P("group", None, "tp"),
            P("group", None, "tp"),
            P("group", None, "tp"),
        ),
        out_specs=P("group", "tp"),
        check_vma=False,
    )
```

profile of v0, /device:TPU:0, one launch (start us, length us, event | category | flops | bytes accessed | tf_op | source)
XLA Modules:
  0.0 114.9 jit_solution(10354878016361298631)
XLA Ops:
  0.0 7.5 %all-to-all-start = ((bf16[16,8,512]{2,1,0:T(8,128)(2,1)}), bf16[16,8,512]{2,1,0:T(8,128)(2,1)S(1)}, u32[]{:S(2)}, u32[]{:S(2)}) async-start(bf16[16,8,512]{2,1,0:T(8,128)(2,1)} %bitcast.117), calls=%async_computation | async-start | bytes 262144 | tf_op jit(solution)/shard_map/all_to_all | solution.py:267
  10.0 3.4 %shard_map.145 = (bf16[1024,128]{1,0:T(8,128)(2,1)S(1)}, f32[1024,128]{1,0:T(8,128)S(1)}) custom-call(f32[16]{0:T(128)S(1)} %copy-done, bf16[64,1024]{1,0:T(8,128)(2,1)} %query_ref.1, bf16[64,512]{1,0:T(8,128)(2,1)} %kv_ref.1, bf16[256,512]{1,0:T(8,128)(2,1)} %local_ref.1, f32[64,128]{1,0:T(8,128)S(1)} %get-tuple-element.80.cos_ref, ...), custom_call_target="tpu_custom_call" | custom-call | tf_op jit(solution)/shard_map/pallas_call | solution.py:292
  14.2 1.2 %all-to-all-done = bf16[16,8,512]{2,1,0:T(8,128)(2,1)S(1)} async-done(((bf16[16,8,512]{2,1,0:T(8,128)(2,1)}), bf16[16,8,512]{2,1,0:T(8,128)(2,1)S(1)}, u32[]{:S(2)}, u32[]{:S(2)}) %all-to-all-start) | async-done | bytes 131104 | tf_op jit(solution)/shard_map/all_to_all | solution.py:267
  15.5 4.0 %shard_map.146 = (bf16[64,1024]{1,0:T(8,128)(2,1)S(1)}, bf16[64,1440]{1,0:T(8,128)(2,1)S(1)}) custom-call(s32[1]{0:T(128)} %bitcast.me_ref, bf16[2,1440,1024]{2,1,0:T(8,128)(2,1)} %bitcast.105, bf16[1024,128]{1,0:T(8,128)(2,1)S(1)} %get-tuple-element.31.rotated_ref, f32[1024,128]{1,0:T(8,128)S(1)} %get-tuple-element.32.state_ref, ...), custom_call_target="tpu_custom_call" | custom-call | tf_op jit(solution)/shard_map/pallas_call | solution.py:226
  19.5 1.6 %collective-permute-start = (bf16[64,1440]{1,0:T(8,128)(2,1)S(1)}, bf16[64,1440]{1,0:T(8,128)(2,1)S(1)}, u32[]{:S(2)}, u32[]{:S(2)}) collective-permute-start(bf16[64,1440]{1,0:T(8,128)(2,1)S(1)} %get-tuple-element.37), channel_id=1, source_target_pairs={{0,1},{1,0},{2,3},{3,2},{4,5},{5,4},{6,7},{7,6},{8,9},{9,8},{10,11... | collective-permute-start | bytes 552968 | tf_op jit(solution)/shard_map/ppermute | solution.py:25
  21.9 2.9 %shard_map.147 = (f32[64,1440]{1,0:T(8,128)S(1)}, bf16[64,1440]{1,0:T(8,128)(2,1)S(1)}) custom-call(s32[1]{0:T(128)} %bitcast.me_ref, bf16[2,1440,1024]{2,1,0:T(8,128)(2,1)} %bitcast.106, bf16[64,1440]{1,0:T(8,128)(2,1)} %residual_ref.1, bf16[64,1024]{1,0:T(8,128)(2,1)S(1)} %get-tuple-element.35.attended_ref), custom_call_target="tpu_custom_call" | custom-call | tf_op jit(solution)/shard_map/pallas_call | solution.py:226
  25.7 2.5 %collective-permute-start.4 = (bf16[64,1440]{1,0:T(8,128)(2,1)S(1)}, bf16[64,1440]{1,0:T(8,128)(2,1)S(1)}, u32[]{:S(2)}, u32[]{:S(2)}) collective-permute-start(bf16[64,1440]{1,0:T(8,128)(2,1)S(1)} %fusion.4), channel_id=1, source_target_pairs={{0,16},{2,18},{4,20},{6,22},{8,24},{10,26},{12,28},{14,30},{16,0},... | collective-permute-start | bytes 552968 | tf_op jit(solution)/shard_map/ppermute | solution.py:25
  28.2 1.5 %collective-permute-start.1 = (bf16[64,1440]{1,0:T(8,128)(2,1)S(1)}, bf16[64,1440]{1,0:T(8,128)(2,1)S(1)}, u32[]{:S(2)}, u32[]{:S(2)}) collective-permute-start(bf16[64,1440]{1,0:T(8,128)(2,1)S(1)} %get-tuple-element.40), channel_id=1, source_target_pairs={{0,1},{1,0},{2,3},{3,2},{4,5},{5,4},{6,7},{7,6},{8,9},{9,8},{10,11... | collective-permute-start | bytes 552968 | tf_op jit(solution)/shard_map/ppermute | solution.py:25
  29.9 4.1 %collective-permute-done.1 = bf16[64,1440]{1,0:T(8,128)(2,1)S(1)} collective-permute-done((bf16[64,1440]{1,0:T(8,128)(2,1)S(1)}, bf16[64,1440]{1,0:T(8,128)(2,1)S(1)}, u32[]{:S(2)}, u32[]{:S(2)}) %collective-permute-start.1) | collective-permute-done | bytes 184352 | tf_op jit(solution)/shard_map/ppermute | solution.py:25
  34.4 1.5 %collective-permute-start.3 = (bf16[2,40,1440]{2,1,0:T(8,128)(2,1)S(1)}, bf16[2,40,1440]{2,1,0:T(8,128)(2,1)S(1)}, u32[]{:S(2)}, u32[]{:S(2)}) collective-permute-start(bf16[2,40,1440]{2,1,0:T(8,128)(2,1)S(1)} %get-tuple-element.63), channel_id=1, source_target_pairs={{0,4},{2,6},{4,0},{6,2},{8,12},{10,14},{12,8},{14,10},{16,20},{18,... | collective-permute-start | bytes 691208 | tf_op jit(solution)/shard_map/ppermute | solution.py:25
  36.6 1.5 %collective-permute-start.7 = (bf16[2,40,1440]{2,1,0:T(8,128)(2,1)S(1)}, bf16[2,40,1440]{2,1,0:T(8,128)(2,1)S(1)}, u32[]{:S(2)}, u32[]{:S(2)}) collective-permute-start(bf16[2,40,1440]{2,1,0:T(8,128)(2,1)S(1)} %get-tuple-element.61), channel_id=1, source_target_pairs={{0,12},{2,14},{4,8},{6,10},{8,4},{10,6},{12,0},{14,2},{16,28},{18,... | collective-permute-start | bytes 691208 | tf_op jit(solution)/shard_map/ppermute | solution.py:25
  38.4 1.5 %collective-permute-start.5 = (bf16[64,1440]{1,0:T(8,128)(2,1)S(1)}, bf16[64,1440]{1,0:T(8,128)(2,1)S(1)}, u32[]{:S(2)}, u32[]{:S(2)}) collective-permute-start(bf16[64,1440]{1,0:T(8,128)(2,1)S(1)} %collective-permute-done.4), channel_id=1, source_target_pairs={{0,1},{1,0},{2,3},{3,2},{4,5},{5,4},{6,7},{7,6},{8,9},{9,8},{10,11... | collective-permute-start | bytes 552968 | tf_op jit(solution)/shard_map/ppermute | solution.py:25
  40.6 4.7 %collective-permute-done.3 = bf16[2,40,1440]{2,1,0:T(8,128)(2,1)S(1)} collective-permute-done((bf16[2,40,1440]{2,1,0:T(8,128)(2,1)S(1)}, bf16[2,40,1440]{2,1,0:T(8,128)(2,1)S(1)}, u32[]{:S(2)}, u32[]{:S(2)}) %collective-permute-start.3) | collective-permute-done | bytes 230432 | tf_op jit(solution)/shard_map/ppermute | solution.py:25
  46.2 1.2 %collective-permute-done.6 = bf16[2,40,1440]{2,1,0:T(8,128)(2,1)S(1)} collective-permute-done((bf16[2,40,1440]{2,1,0:T(8,128)(2,1)S(1)}, bf16[2,40,1440]{2,1,0:T(8,128)(2,1)S(1)}, u32[]{:S(2)}, u32[]{:S(2)}) %collective-permute-start.6) | collective-permute-done | bytes 230432 | tf_op jit(solution)/shard_map/ppermute | solution.py:25
  47.7 2.4 %collective-permute-start.11 = (bf16[2,40,1440]{2,1,0:T(8,128)(2,1)S(1)}, bf16[2,40,1440]{2,1,0:T(8,128)(2,1)S(1)}, u32[]{:S(2)}, u32[]{:S(2)}) collective-permute-start(bf16[2,40,1440]{2,1,0:T(8,128)(2,1)S(1)} %get-tuple-element.57), channel_id=1, source_target_pairs={{0,12},{2,14},{4,8},{6,10},{8,4},{10,6},{12,0},{14,2},{16,28},{18,... | collective-permute-start | bytes 691208 | tf_op jit(solution)/shard_map/ppermute | solution.py:25
  51.2 5.9 %shard_map.148.refs_0_ = bf16[320,720]{1,0:T(8,128)(2,1)S(1)} custom-call(s32[1]{0:T(128)} %bitcast.me_ref, bf16[720,2880]{1,0:T(8,128)(2,1)} %bitcast.109, bf16[720,2880]{1,0:T(8,128)(2,1)} %bitcast.111, f32[1,2880]{1,0:T(1,128)} %reshape.147.gain_ref, bf16[2,160,1440]{2,1,0:T(8,128)(2,1)S(1)} %constant_dynamic-update-slice_fusion.refs_0_, ...), custom_call_target="tpu_custom_call" | custom-call | tf_op jit(solution)/shard_map/pallas_call | solution.py:226
  57.4 5.2 %collective-permute-done.10 = bf16[2,40,1440]{2,1,0:T(8,128)(2,1)S(1)} collective-permute-done((bf16[2,40,1440]{2,1,0:T(8,128)(2,1)S(1)}, bf16[2,40,1440]{2,1,0:T(8,128)(2,1)S(1)}, u32[]{:S(2)}, u32[]{:S(2)}) %collective-permute-start.10) | collective-permute-done | bytes 230432 | tf_op jit(solution)/shard_map/ppermute | solution.py:25
  62.8 1.6 %collective-permute-start.13 = (bf16[320,720]{1,0:T(8,128)(2,1)S(1)}, bf16[320,720]{1,0:T(8,128)(2,1)S(1)}, u32[]{:S(2)}, u32[]{:S(2)}) collective-permute-start(bf16[320,720]{1,0:T(8,128)(2,1)S(1)} %shard_map.148.refs_0_), channel_id=1, source_target_pairs={{0,1},{1,0},{2,3},{3,2},{4,5},{5,4},{6,7},{7,6},{8,9},{9,8},{10,11... | collective-permute-start | bytes 1382408 | tf_op jit(solution)/shard_map/ppermute | solution.py:25
  65.3 6.1 %shard_map.149.refs_0_ = bf16[320,720]{1,0:T(8,128)(2,1)S(1)} custom-call(s32[1]{0:T(128)} %bitcast.me_ref, bf16[720,2880]{1,0:T(8,128)(2,1)} %bitcast.110, bf16[720,2880]{1,0:T(8,128)(2,1)} %bitcast.112, f32[1,2880]{1,0:T(1,128)} %reshape.147.gain_ref, bf16[2,160,1440]{2,1,0:T(8,128)(2,1)S(1)} %constant_dynamic-update-slice_fusion.4.refs_0_, ...), custom_call_target="tpu_custom_call" | custom-call | tf_op jit(solution)/shard_map/pallas_call | solution.py:226
  71.4 1.6 %collective-permute-start.18 = (bf16[320,720]{1,0:T(8,128)(2,1)S(1)}, bf16[320,720]{1,0:T(8,128)(2,1)S(1)}, u32[]{:S(2)}, u32[]{:S(2)}) collective-permute-start(bf16[320,720]{1,0:T(8,128)(2,1)S(1)} %shard_map.149.refs_0_), channel_id=1, source_target_pairs={{0,1},{1,0},{2,3},{3,2},{4,5},{5,4},{6,7},{7,6},{8,9},{9,8},{10,11... | collective-permute-start | bytes 1382408 | tf_op jit(solution)/shard_map/ppermute | solution.py:25
  73.0 3.9 %collective-permute-done.13.refs_1_ = bf16[320,720]{1,0:T(8,128)(2,1)S(1)} collective-permute-done((bf16[320,720]{1,0:T(8,128)(2,1)S(1)}, bf16[320,720]{1,0:T(8,128)(2,1)S(1)}, u32[]{:S(2)}, u32[]{:S(2)}) %collective-permute-start.13) | collective-permute-done | bytes 460832 | tf_op jit(solution)/shard_map/ppermute | solution.py:25
  76.9 3.5 %shard_map.150 = (bf16[160,1440]{1,0:T(8,128)(2,1)S(1)}, bf16[160,1440]{1,0:T(8,128)(2,1)S(1)}) custom-call(s32[1]{0:T(128)} %bitcast.me_ref, bf16[2,720,1440]{2,1,0:T(8,128)(2,1)} %bitcast.107, bf16[320,720]{1,0:T(8,128)(2,1)S(1)} %shard_map.148.refs_0_, bf16[320,720]{1,0:T(8,128)(2,1)S(1)} %collective-permute-done.13.refs_1_), custom_call_target="tpu_custom_call" | custom-call | tf_op jit(solution)/shard_map/pallas_call | solution.py:226
  80.7 6.2 %collective-permute-done.18.refs_1_ = bf16[320,720]{1,0:T(8,128)(2,1)S(1)} collective-permute-done((bf16[320,720]{1,0:T(8,128)(2,1)S(1)}, bf16[320,720]{1,0:T(8,128)(2,1)S(1)}, u32[]{:S(2)}, u32[]{:S(2)}) %collective-permute-start.18) | collective-permute-done | bytes 460832 | tf_op jit(solution)/shard_map/ppermute | solution.py:25
  86.9 3.5 %shard_map.151 = (bf16[160,1440]{1,0:T(8,128)(2,1)S(1)}, bf16[160,1440]{1,0:T(8,128)(2,1)S(1)}) custom-call(s32[1]{0:T(128)} %bitcast.me_ref, bf16[2,720,1440]{2,1,0:T(8,128)(2,1)} %bitcast.108, bf16[320,720]{1,0:T(8,128)(2,1)S(1)} %shard_map.149.refs_0_, bf16[320,720]{1,0:T(8,128)(2,1)S(1)} %collective-permute-done.18.refs_1_), custom_call_target="tpu_custom_call" | custom-call | tf_op jit(solution)/shard_map/pallas_call | solution.py:226
  90.7 1.7 %collective-permute-done.19 = bf16[160,1440]{1,0:T(8,128)(2,1)S(1)} collective-permute-done((bf16[160,1440]{1,0:T(8,128)(2,1)S(1)}, bf16[160,1440]{1,0:T(8,128)(2,1)S(1)}, u32[]{:S(2)}, u32[]{:S(2)}) %collective-permute-start.19) | collective-permute-done | bytes 460832 | tf_op jit(solution)/shard_map/ppermute | solution.py:25
  92.5 1.5 %collective-permute-start.20 = (bf16[40,1440]{1,0:T(8,128)(2,1)S(1)}, bf16[40,1440]{1,0:T(8,128)(2,1)S(1)}, u32[]{:S(2)}, u32[]{:S(2)}) collective-permute-start(bf16[40,1440]{1,0:T(8,128)(2,1)S(1)} %get-tuple-element.68), channel_id=1, source_target_pairs={{0,4},{2,6},{4,0},{6,2},{8,12},{10,14},{12,8},{14,10},{16,20},{18,... | collective-permute-start | bytes 345608 | tf_op jit(solution)/shard_map/ppermute | solution.py:25
  96.1 1.5 %collective-permute-start.15 = (bf16[40,1440]{1,0:T(8,128)(2,1)S(1)}, bf16[40,1440]{1,0:T(8,128)(2,1)S(1)}, u32[]{:S(2)}, u32[]{:S(2)}) collective-permute-start(bf16[40,1440]{1,0:T(8,128)(2,1)S(1)} %get-tuple-element.72), channel_id=1, source_target_pairs={{0,4},{2,6},{4,0},{6,2},{8,12},{10,14},{12,8},{14,10},{16,20},{18,... | collective-permute-start | bytes 345608 | tf_op jit(solution)/shard_map/ppermute | solution.py:25
  100.2 2.6 %collective-permute-done.22 = bf16[40,1440]{1,0:T(8,128)(2,1)S(1)} collective-permute-done((bf16[40,1440]{1,0:T(8,128)(2,1)S(1)}, bf16[40,1440]{1,0:T(8,128)(2,1)S(1)}, u32[]{:S(2)}, u32[]{:S(2)}) %collective-permute-start.22) | collective-permute-done | bytes 115232 | tf_op jit(solution)/shard_map/ppermute | solution.py:25
  103.3 2.3 %collective-permute-start.23 = (bf16[64,1440]{1,0:T(8,128)(2,1)S(1)}, bf16[64,1440]{1,0:T(8,128)(2,1)S(1)}, u32[]{:S(2)}, u32[]{:S(2)}) collective-permute-start(bf16[64,1440]{1,0:T(8,128)(2,1)S(1)} %fusion.3), channel_id=1, source_target_pairs={{0,16},{2,18},{4,20},{6,22},{8,24},{10,26},{12,28},{14,30},{16,0},... | collective-permute-start | bytes 552968 | tf_op jit(solution)/shard_map/ppermute | solution.py:25
  105.6 2.0 %collective-permute-done.16 = bf16[40,1440]{1,0:T(8,128)(2,1)S(1)} collective-permute-done((bf16[40,1440]{1,0:T(8,128)(2,1)S(1)}, bf16[40,1440]{1,0:T(8,128)(2,1)S(1)}, u32[]{:S(2)}, u32[]{:S(2)}) %collective-permute-start.16) | collective-permute-done | bytes 115232 | tf_op jit(solution)/shard_map/ppermute | solution.py:25
  107.6 1.9 %collective-permute-done.17 = bf16[40,1440]{1,0:T(8,128)(2,1)S(1)} collective-permute-done((bf16[40,1440]{1,0:T(8,128)(2,1)S(1)}, bf16[40,1440]{1,0:T(8,128)(2,1)S(1)}, u32[]{:S(2)}, u32[]{:S(2)}) %collective-permute-start.17) | collective-permute-done | bytes 115232 | tf_op jit(solution)/shard_map/ppermute | solution.py:25
  109.8 4.2 %collective-permute-done.23 = bf16[64,1440]{1,0:T(8,128)(2,1)S(1)} collective-permute-done((bf16[64,1440]{1,0:T(8,128)(2,1)S(1)}, bf16[64,1440]{1,0:T(8,128)(2,1)S(1)}, u32[]{:S(2)}, u32[]{:S(2)}) %collective-permute-start.23) | collective-permute-done | bytes 184352 | tf_op jit(solution)/shard_map/ppermute | solution.py:25
  (80 shorter events, 17.4 us)
Async XLA Ops:
  0.0 21.3 %copy-start.1 = (f32[2880]{0:T(1024)S(1)}, f32[2880]{0:T(1024)}, u32[]{:S(2)}) copy-start(f32[2880]{0:T(1024)} %param.24) | copy-start | bytes 34564
  0.0 15.5 %all-to-all-start = ((bf16[16,8,512]{2,1,0:T(8,128)(2,1)}), bf16[16,8,512]{2,1,0:T(8,128)(2,1)S(1)}, u32[]{:S(2)}, u32[]{:S(2)}) async-start(bf16[16,8,512]{2,1,0:T(8,128)(2,1)} %bitcast.117), calls=%async_computation | async-start | bytes 262144 | tf_op jit(solution)/shard_map/all_to_all | solution.py:267
  9.4 0.7 copy-start
  19.4 5.3 %copy-start.2 = (f32[64,4]{0,1:T(4,128)S(1)}, f32[64,4]{0,1:T(4,128)}, u32[]{:S(2)}) copy-start(f32[64,4]{0,1:T(4,128)} %param.26) | copy-start | bytes 3076
  19.5 6.2 %collective-permute-start = (bf16[64,1440]{1,0:T(8,128)(2,1)S(1)}, bf16[64,1440]{1,0:T(8,128)(2,1)S(1)}, u32[]{:S(2)}, u32[]{:S(2)}) collective-permute-start(bf16[64,1440]{1,0:T(8,128)(2,1)S(1)} %get-tuple-element.37), channel_id=1, source_target_pairs={{0,1},{1,0},{2,3},{3,2},{4,5},{5,4},{6,7},{7,6},{8,9},{9,8},{10,11... | collective-permute-start | bytes 552968 | tf_op jit(solution)/shard_map/ppermute | solution.py:25
  25.7 12.7 %collective-permute-start.4 = (bf16[64,1440]{1,0:T(8,128)(2,1)S(1)}, bf16[64,1440]{1,0:T(8,128)(2,1)S(1)}, u32[]{:S(2)}, u32[]{:S(2)}) collective-permute-start(bf16[64,1440]{1,0:T(8,128)(2,1)S(1)} %fusion.4), channel_id=1, source_target_pairs={{0,16},{2,18},{4,20},{6,22},{8,24},{10,26},{12,28},{14,30},{16,0},... | collective-permute-start | bytes 552968 | tf_op jit(solution)/shard_map/ppermute | solution.py:25
  28.2 5.9 %collective-permute-start.1 = (bf16[64,1440]{1,0:T(8,128)(2,1)S(1)}, bf16[64,1440]{1,0:T(8,128)(2,1)S(1)}, u32[]{:S(2)}, u32[]{:S(2)}) collective-permute-start(bf16[64,1440]{1,0:T(8,128)(2,1)S(1)} %get-tuple-element.40), channel_id=1, source_target_pairs={{0,1},{1,0},{2,3},{3,2},{4,5},{5,4},{6,7},{7,6},{8,9},{9,8},{10,11... | collective-permute-start | bytes 552968 | tf_op jit(solution)/shard_map/ppermute | solution.py:25
  34.4 10.9 %collective-permute-start.3 = (bf16[2,40,1440]{2,1,0:T(8,128)(2,1)S(1)}, bf16[2,40,1440]{2,1,0:T(8,128)(2,1)S(1)}, u32[]{:S(2)}, u32[]{:S(2)}) collective-permute-start(bf16[2,40,1440]{2,1,0:T(8,128)(2,1)S(1)} %get-tuple-element.63), channel_id=1, source_target_pairs={{0,4},{2,6},{4,0},{6,2},{8,12},{10,14},{12,8},{14,10},{16,20},{18,... | collective-permute-start | bytes 691208 | tf_op jit(solution)/shard_map/ppermute | solution.py:25
  36.0 4.7 %collective-permute-start.2 = (f32[64,8]{0,1:T(8,128)S(1)}, f32[64,8]{0,1:T(8,128)S(1)}, u32[]{:S(2)}, u32[]{:S(2)}) collective-permute-start(f32[64,8]{0,1:T(8,128)S(1)} %pad_maximum_fusion.8), channel_id=1, source_target_pairs={{0,16},{2,18},{4,20},{6,22},{8,24},{10,26},{12,28},{14,30},{16,0},... | collective-permute-start | bytes 6152 | tf_op jit(solution)/shard_map/ppermute | solution.py:25
  36.6 9.6 %collective-permute-start.7 = (bf16[2,40,1440]{2,1,0:T(8,128)(2,1)S(1)}, bf16[2,40,1440]{2,1,0:T(8,128)(2,1)S(1)}, u32[]{:S(2)}, u32[]{:S(2)}) collective-permute-start(bf16[2,40,1440]{2,1,0:T(8,128)(2,1)S(1)} %get-tuple-element.61), channel_id=1, source_target_pairs={{0,12},{2,14},{4,8},{6,10},{8,4},{10,6},{12,0},{14,2},{16,28},{18,... | collective-permute-start | bytes 691208 | tf_op jit(solution)/shard_map/ppermute | solution.py:25
  38.1 9.3 %collective-permute-start.6 = (bf16[2,40,1440]{2,1,0:T(8,128)(2,1)S(1)}, bf16[2,40,1440]{2,1,0:T(8,128)(2,1)S(1)}, u32[]{:S(2)}, u32[]{:S(2)}) collective-permute-start(bf16[2,40,1440]{2,1,0:T(8,128)(2,1)S(1)} %get-tuple-element.64), channel_id=1, source_target_pairs={{0,8},{2,10},{4,12},{6,14},{8,0},{10,2},{12,4},{14,6},{16,24},{18,... | collective-permute-start | bytes 691208 | tf_op jit(solution)/shard_map/ppermute | solution.py:25
  38.4 7.5 %collective-permute-start.5 = (bf16[64,1440]{1,0:T(8,128)(2,1)S(1)}, bf16[64,1440]{1,0:T(8,128)(2,1)S(1)}, u32[]{:S(2)}, u32[]{:S(2)}) collective-permute-start(bf16[64,1440]{1,0:T(8,128)(2,1)S(1)} %collective-permute-done.4), channel_id=1, source_target_pairs={{0,1},{1,0},{2,3},{3,2},{4,5},{5,4},{6,7},{7,6},{8,9},{9,8},{10,11... | collective-permute-start | bytes 552968 | tf_op jit(solution)/shard_map/ppermute | solution.py:25
  47.5 3.7 %collective-permute-start.8 = (bf16[2,160,1440]{2,1,0:T(8,128)(2,1)S(1)}, bf16[2,160,1440]{2,1,0:T(8,128)(2,1)S(1)}, u32[]{:S(2)}, u32[]{:S(2)}) collective-permute-start(bf16[2,160,1440]{2,1,0:T(8,128)(2,1)S(1)} %constant_dynamic-update-slice_fusion.refs_0_), channel_id=1, source_target_pairs={{0,2},{2,0},{4,6},{6,4},{8,10},{10,8},{12,14},{14,12},{16,18},{18,... | collective-permute-start | bytes 2764808 | tf_op jit(solution)/shard_map/ppermute | solution.py:25
  47.7 9.8 %collective-permute-start.11 = (bf16[2,40,1440]{2,1,0:T(8,128)(2,1)S(1)}, bf16[2,40,1440]{2,1,0:T(8,128)(2,1)S(1)}, u32[]{:S(2)}, u32[]{:S(2)}) collective-permute-start(bf16[2,40,1440]{2,1,0:T(8,128)(2,1)S(1)} %get-tuple-element.57), channel_id=1, source_target_pairs={{0,12},{2,14},{4,8},{6,10},{8,4},{10,6},{12,0},{14,2},{16,28},{18,... | collective-permute-start | bytes 691208 | tf_op jit(solution)/shard_map/ppermute | solution.py:25
  50.0 12.6 %collective-permute-start.10 = (bf16[2,40,1440]{2,1,0:T(8,128)(2,1)S(1)}, bf16[2,40,1440]{2,1,0:T(8,128)(2,1)S(1)}, u32[]{:S(2)}, u32[]{:S(2)}) collective-permute-start(bf16[2,40,1440]{2,1,0:T(8,128)(2,1)S(1)} %get-tuple-element.60), channel_id=1, source_target_pairs={{0,8},{2,10},{4,12},{6,14},{8,0},{10,2},{12,4},{14,6},{16,24},{18,... | collective-permute-start | bytes 691208 | tf_op jit(solution)/shard_map/ppermute | solution.py:25
  51.0 11.6 %collective-permute-start.9 = (bf16[2,40,1440]{2,1,0:T(8,128)(2,1)S(1)}, bf16[2,40,1440]{2,1,0:T(8,128)(2,1)S(1)}, u32[]{:S(2)}, u32[]{:S(2)}) collective-permute-start(bf16[2,40,1440]{2,1,0:T(8,128)(2,1)S(1)} %get-tuple-element.59), channel_id=1, source_target_pairs={{0,4},{2,6},{4,0},{6,2},{8,12},{10,14},{12,8},{14,10},{16,20},{18,... | collective-permute-start | bytes 691208 | tf_op jit(solution)/shard_map/ppermute | solution.py:25
  62.7 2.6 %collective-permute-start.12 = (bf16[2,160,1440]{2,1,0:T(8,128)(2,1)S(1)}, bf16[2,160,1440]{2,1,0:T(8,128)(2,1)S(1)}, u32[]{:S(2)}, u32[]{:S(2)}) collective-permute-start(bf16[2,160,1440]{2,1,0:T(8,128)(2,1)S(1)} %constant_dynamic-update-slice_fusion.4.refs_0_), channel_id=1, source_target_pairs={{0,2},{2,0},{4,6},{6,4},{8,10},{10,8},{12,14},{14,12},{16,18},{18,... | collective-permute-start | bytes 2764808 | tf_op jit(solution)/shard_map/ppermute | solution.py:25
  62.8 14.1 %collective-permute-start.13 = (bf16[320,720]{1,0:T(8,128)(2,1)S(1)}, bf16[320,720]{1,0:T(8,128)(2,1)S(1)}, u32[]{:S(2)}, u32[]{:S(2)}) collective-permute-start(bf16[320,720]{1,0:T(8,128)(2,1)S(1)} %shard_map.148.refs_0_), channel_id=1, source_target_pairs={{0,1},{1,0},{2,3},{3,2},{4,5},{5,4},{6,7},{7,6},{8,9},{9,8},{10,11... | collective-permute-start | bytes 1382408 | tf_op jit(solution)/shard_map/ppermute | solution.py:25
  71.4 15.5 %collective-permute-start.18 = (bf16[320,720]{1,0:T(8,128)(2,1)S(1)}, bf16[320,720]{1,0:T(8,128)(2,1)S(1)}, u32[]{:S(2)}, u32[]{:S(2)}) collective-permute-start(bf16[320,720]{1,0:T(8,128)(2,1)S(1)} %shard_map.149.refs_0_), channel_id=1, source_target_pairs={{0,1},{1,0},{2,3},{3,2},{4,5},{5,4},{6,7},{7,6},{8,9},{9,8},{10,11... | collective-permute-start | bytes 1382408 | tf_op jit(solution)/shard_map/ppermute | solution.py:25
  80.4 10.2 %collective-permute-start.14 = (bf16[160,1440]{1,0:T(8,128)(2,1)S(1)}, bf16[160,1440]{1,0:T(8,128)(2,1)S(1)}, u32[]{:S(2)}, u32[]{:S(2)}) collective-permute-start(bf16[160,1440]{1,0:T(8,128)(2,1)S(1)} %get-tuple-element.53), channel_id=1, source_target_pairs={{0,2},{2,0},{4,6},{6,4},{8,10},{10,8},{12,14},{14,12},{16,18},{18,... | collective-permute-start | bytes 1382408 | tf_op jit(solution)/shard_map/ppermute | solution.py:25
  90.5 1.9 %collective-permute-start.19 = (bf16[160,1440]{1,0:T(8,128)(2,1)S(1)}, bf16[160,1440]{1,0:T(8,128)(2,1)S(1)}, u32[]{:S(2)}, u32[]{:S(2)}) collective-permute-start(bf16[160,1440]{1,0:T(8,128)(2,1)S(1)} %get-tuple-element.56), channel_id=1, source_target_pairs={{0,2},{2,0},{4,6},{6,4},{8,10},{10,8},{12,14},{14,12},{16,18},{18,... | collective-permute-start | bytes 1382408 | tf_op jit(solution)/shard_map/ppermute | solution.py:25
  92.5 6.2 %collective-permute-start.20 = (bf16[40,1440]{1,0:T(8,128)(2,1)S(1)}, bf16[40,1440]{1,0:T(8,128)(2,1)S(1)}, u32[]{:S(2)}, u32[]{:S(2)}) collective-permute-start(bf16[40,1440]{1,0:T(8,128)(2,1)S(1)} %get-tuple-element.68), channel_id=1, source_target_pairs={{0,4},{2,6},{4,0},{6,2},{8,12},{10,14},{12,8},{14,10},{16,20},{18,... | collective-permute-start | bytes 345608 | tf_op jit(solution)/shard_map/ppermute | solution.py:25
  94.0 6.2 %collective-permute-start.21 = (bf16[40,1440]{1,0:T(8,128)(2,1)S(1)}, bf16[40,1440]{1,0:T(8,128)(2,1)S(1)}, u32[]{:S(2)}, u32[]{:S(2)}) collective-permute-start(bf16[40,1440]{1,0:T(8,128)(2,1)S(1)} %get-tuple-element.67), channel_id=1, source_target_pairs={{0,8},{2,10},{4,12},{6,14},{8,0},{10,2},{12,4},{14,6},{16,24},{18,... | collective-permute-start | bytes 345608 | tf_op jit(solution)/shard_map/ppermute | solution.py:25
  95.1 7.7 %collective-permute-start.22 = (bf16[40,1440]{1,0:T(8,128)(2,1)S(1)}, bf16[40,1440]{1,0:T(8,128)(2,1)S(1)}, u32[]{:S(2)}, u32[]{:S(2)}) collective-permute-start(bf16[40,1440]{1,0:T(8,128)(2,1)S(1)} %get-tuple-element.66), channel_id=1, source_target_pairs={{0,12},{2,14},{4,8},{6,10},{8,4},{10,6},{12,0},{14,2},{16,28},{18,... | collective-permute-start | bytes 345608 | tf_op jit(solution)/shard_map/ppermute | solution.py:25
  96.1 9.5 %collective-permute-start.15 = (bf16[40,1440]{1,0:T(8,128)(2,1)S(1)}, bf16[40,1440]{1,0:T(8,128)(2,1)S(1)}, u32[]{:S(2)}, u32[]{:S(2)}) collective-permute-start(bf16[40,1440]{1,0:T(8,128)(2,1)S(1)} %get-tuple-element.72), channel_id=1, source_target_pairs={{0,4},{2,6},{4,0},{6,2},{8,12},{10,14},{12,8},{14,10},{16,20},{18,... | collective-permute-start | bytes 345608 | tf_op jit(solution)/shard_map/ppermute | solution.py:25
  97.6 10.0 %collective-permute-start.16 = (bf16[40,1440]{1,0:T(8,128)(2,1)S(1)}, bf16[40,1440]{1,0:T(8,128)(2,1)S(1)}, u32[]{:S(2)}, u32[]{:S(2)}) collective-permute-start(bf16[40,1440]{1,0:T(8,128)(2,1)S(1)} %get-tuple-element.71), channel_id=1, source_target_pairs={{0,8},{2,10},{4,12},{6,14},{8,0},{10,2},{12,4},{14,6},{16,24},{18,... | collective-permute-start | bytes 345608 | tf_op jit(solution)/shard_map/ppermute | solution.py:25
  98.7 10.8 %collective-permute-start.17 = (bf16[40,1440]{1,0:T(8,128)(2,1)S(1)}, bf16[40,1440]{1,0:T(8,128)(2,1)S(1)}, u32[]{:S(2)}, u32[]{:S(2)}) collective-permute-start(bf16[40,1440]{1,0:T(8,128)(2,1)S(1)} %get-tuple-element.70), channel_id=1, source_target_pairs={{0,12},{2,14},{4,8},{6,10},{8,4},{10,6},{12,0},{14,2},{16,28},{18,... | collective-permute-start | bytes 345608 | tf_op jit(solution)/shard_map/ppermute | solution.py:25
  103.3 10.7 %collective-permute-start.23 = (bf16[64,1440]{1,0:T(8,128)(2,1)S(1)}, bf16[64,1440]{1,0:T(8,128)(2,1)S(1)}, u32[]{:S(2)}, u32[]{:S(2)}) collective-permute-start(bf16[64,1440]{1,0:T(8,128)(2,1)S(1)} %fusion.3), channel_id=1, source_target_pairs={{0,16},{2,18},{4,20},{6,22},{8,24},{10,26},{12,28},{14,30},{16,0},... | collective-permute-start | bytes 552968 | tf_op jit(solution)/shard_map/ppermute | solution.py:25
where the time goes:
time: 115 us
  waiting for transfers between devices  42.1 us (37%)
  starting transfers between devices  35.1 us (31%)
  Pallas kernels  29.3 us (25%)
  matrix products  2.95 us (3%)
  other arithmetic  2.73 us (2%)
  local copies, waits for them, and re-layouts  1.66 us (1%)
    ppermute x24, waiting for transfers between devices, exchange(): return lax.ppermute(value, axis, [(i, i ^ offset) for i in range(size)])  40.9 us
    ppermute x24, starting transfers between devices, exchange(): return lax.ppermute(value, axis, [(i, i ^ offset) for i in range(size)])  27.6 us
    pallas_call x6, Pallas kernels, kernel_call(): pl.pallas_call(kernel, out_shape=[pltpu.VMEM(shape, dtype) for shape, dty...  25.9 us
    all_to_all x1, starting transfers between devices, on_device(): lax.all_to_all(remote_pool.reshape(groups, -1, lane_count), 'group', spli...  7.52 us
    pallas_call x1, Pallas kernels, on_device(): pl.pallas_call(local_kernel, out_shape=[pltpu.VMEM((states, 2 * HEAD), jn...  3.41 us
  transfers between devices with their start and end apart: 25, of which 17 were waited for; matrix products, arithmetic and copies ran while one was open for 5% of the time, Pallas kernels for 22%

commit v1 on v0

--- a/solution.py
+++ b/solution.py
@@ -9,7 +9,6 @@
 
 HEAD = 64
 TILE = 256
-PARTS = 1
 VMEM_LIMIT = 24 * 1024 * 1024
 
 
@@ -89,19 +88,6 @@
         state_ref[place, :] = jnp.where(lane == 0, row_max, jnp.where(lane == 1, denominator, blended))
 
 
-def split_copies(source, target, sems, first, parts):
-    rows = source.shape[0]
-    step = rows if parts == 1 else -(-rows // parts) // 16 * 16 + 16
-    return [
-        pltpu.make_async_copy(
-            source.at[start : min(start + step, rows)],
-            target.at[start : min(start + step, rows)],
-            sems.at[first + i],
-        )
-        for i, start in enumerate(range(0, rows, step))
-    ]
-
-
 def start_all(copies):
     for copy in copies:
         copy.start()
@@ -115,11 +101,10 @@
 def page_kernel(me_ref, weight_ref, rotated_ref, state_ref, page_ref, valid_ref, attended_ref, *refs):
     other_refs, held_ref, sems = refs[:-2], refs[-2], refs[-1]
     copies = [
-        split_copies(weight_ref.at[me_ref[0] ^ (j + 1)], held_ref.at[j], sems, 2 * j, 2)
+        pltpu.make_async_copy(weight_ref.at[me_ref[0] ^ (j + 1)], held_ref.at[j], sems.at[j])
         for j in range(len(other_refs))
     ]
-    for some in copies:
-        start_all(some)
+    start_all(copies)
     tokens = attended_ref.shape[0]
     pair = 2 * HEAD
     kv_heads = page_ref.shape[1] // pair
@@ -147,15 +132,17 @@
             ).astype(jnp.bfloat16)
     attended = attended_ref[...]
     for j, ref in enumerate(other_refs):
-        wait_all(copies[j])
+        copies[j].wait()
         ref[...] = dot_nt(attended, held_ref[j]).astype(jnp.bfloat16)
 
 
 def own_columns_kernel(
     me_ref, weight_ref, residual_ref, attended_ref, out_ref, sent_ref, held_ref, rows_ref, sems
 ):
-    copies = split_copies(weight_ref.at[me_ref[0]], held_ref, sems, 0, PARTS)
-    copies.append(pltpu.make_async_copy(residual_ref, rows_ref, sems.at[PARTS]))
+    copies = [
+        pltpu.make_async_copy(weight_ref.at[me_ref[0]], held_ref, sems.at[0]),
+        pltpu.make_async_copy(residual_ref, rows_ref, sems.at[1]),
+    ]
     start_all(copies)
     wait_all(copies)
     terms = rows_ref[...].astype(jnp.float32) + dot_nt(attended_ref[...], held_ref[...])
@@ -170,15 +157,18 @@
 def gate_up_kernel(parts, me_ref, gate_ref, up_ref, gain_ref, *refs):
     sets, (out_ref, place_ref, row_ref, gate_held, up_held, gain_held, sems) = refs[:-7], refs[-7:]
     rows, width = sets[0].shape[1:]
-    features, hidden = gate_ref.shape[1], gate_ref.shape[0]
+    blocks, block, features = gate_ref.shape
     gain_copy = pltpu.make_async_copy(gain_ref, gain_held, sems.at[0])
     gain_copy.start()
     copies = []
-    for t, tile in enumerate(tiles(hidden)):
-        some = split_copies(gate_ref.at[tile], gate_held.at[tile], sems, 1 + 4 * t, 2)
-        some += split_copies(up_ref.at[tile], up_held.at[tile], sems, 3 + 4 * t, 2)
-        start_all(some)
-        copies.append(some)
+    for t in range(blocks):
+        copies.append(
+            [
+                pltpu.make_async_copy(gate_ref.at[t], gate_held.at[t], sems.at[1 + 2 * t]),
+                pltpu.make_async_copy(up_ref.at[t], up_held.at[t], sems.at[2 + 2 * t]),
+            ]
+        )
+        start_all(copies[-1])
     me = me_ref[0]
     gain_copy.wait()
     for s, ref in enumerate(sets):
@@ -189,12 +179,12 @@
             place_ref[me ^ j] = held[j] * scale
         whole = jnp.concatenate([place_ref[p] for p in range(parts)], axis=1)
         row_ref[pl.ds(s * rows, rows), :] = (whole * gain_held[...]).astype(jnp.bfloat16)
-    for t, tile in enumerate(tiles(hidden)):
+    for t in range(blocks):
         wait_all(copies[t])
-        gate_val = dot_nt(row_ref[...], gate_held[tile])
-        up_val = dot_nt(row_ref[...], up_held[tile])
+        gate_val = dot_nt(row_ref[...], gate_held[t])
+        up_val = dot_nt(row_ref[...], up_held[t])
         active = gate_val * jax.nn.sigmoid(ALPHA * gate_val) * (up_val + 1.0)
-        out_ref[:, tile] = active.astype(jnp.bfloat16)
+        out_ref[:, t * block : (t + 1) * block] = active.astype(jnp.bfloat16)
 
 
 def down_kernel(me_ref, down_ref, *refs):
@@ -202,13 +192,12 @@
     actives = refs[:-5]
     rows, width = own_ref.shape
     copies = [
-        split_copies(down_ref.at[me_ref[0] ^ j], held_ref.at[j], sems, PARTS * j, PARTS)
+        pltpu.make_async_copy(down_ref.at[me_ref[0] ^ j], held_ref.at[j], sems.at[j])
         for j in range(len(actives))
     ]
-    for some in copies:
-        start_all(some)
+    start_all(copies)
     for j, ref in enumerate(actives):
-        wait_all(copies[j])
+        copies[j].wait()
         for tile in tiles(width):
             term = jnp.dot(ref[...], held_ref[j, :, tile], preferred_element_type=jnp.float32)
             if j > 0:
@@ -284,7 +273,10 @@
     sine = jnp.where(lane < HEAD // 2, -1.0, 1.0)[None, :] * jnp.sin(angles)
     hidden = expert_gate.shape[2]
     weight = out_weight.T.reshape(tp, width, out_weight.shape[0])
-    gate, up = expert_gate[0].T, expert_up[0].T
+    blocks = 3 if hidden % 48 == 0 else 1
+    gate, up = [
+        value[0].T.reshape(blocks, hidden // blocks, tp * width) for value in (expert_gate, expert_up)
+    ]
     down = expert_down.reshape(tp, hidden, width)
     dma = pltpu.SemaphoreType.DMA
     in_vmem = pl.BlockSpec(memory_space=pltpu.VMEM)
@@ -312,7 +304,7 @@
         state,
         fetched.reshape(-1, lane_count),
         page_valid,
-        scratch=[pltpu.VMEM((tp - 1, *weight.shape[1:]), jnp.bfloat16), dma((2 * (tp - 1),))],
+        scratch=[pltpu.VMEM((tp - 1, *weight.shape[1:]), jnp.bfloat16), dma((tp - 1,))],
     )
     arriving = [exchange(other, "tp", j + 1) for j, other in enumerate(others)]
     gain, route_weights, _ = lax.optimization_barrier((norm_gain, route_weights, attended))
@@ -326,7 +318,7 @@
         scratch=[
             pltpu.VMEM(weight.shape[1:], jnp.bfloat16),
             pltpu.VMEM(residual.shape, jnp.bfloat16),
-            dma((PARTS + 1,)),
+            dma((2,)),
         ],
     )
     for term in arriving:
@@ -404,7 +396,7 @@
                 pltpu.VMEM(gate.shape, jnp.bfloat16),
                 pltpu.VMEM(up.shape, jnp.bfloat16),
                 pltpu.VMEM(gain.shape, jnp.float32),
-                dma((1 + 4 * len(tiles(hidden)),)),
+                dma((1 + 2 * blocks,)),
             ],
         )
         return active
@@ -420,7 +412,7 @@
             scratch=[
                 pltpu.VMEM(down.shape, jnp.bfloat16),
                 pltpu.VMEM((2 * rows, width), jnp.float32),
-                dma((PARTS * tp,)),
+                dma((tp,)),
             ],
         )
 

time: 115 us -> 114 us (level)
  no operation moved by 1% of the time
where the time goes in v1:
time: 114 us
  waiting for transfers between devices  41.9 us (37%)
  starting transfers between devices  35.1 us (31%)
  Pallas kernels  28.4 us (25%)
  matrix products  2.96 us (3%)
  other arithmetic  2.73 us (2%)
  local copies, waits for them, and re-layouts  1.66 us (1%)
    ppermute x24, waiting for transfers between devices, exchange(): return lax.ppermute(value, axis, [(i, i ^ offset) for i in range(size)])  40.7 us
    ppermute x24, starting transfers between devices, exchange(): return lax.ppermute(value, axis, [(i, i ^ offset) for i in range(size)])  27.6 us
    pallas_call x6, Pallas kernels, kernel_call(): pl.pallas_call(kernel, out_shape=[pltpu.VMEM(shape, dtype) for shape, dty...  25 us
    all_to_all x1, starting transfers between devices, on_device(): lax.all_to_all(remote_pool.reshape(groups, -1, lane_count), 'group', spli...  7.52 us
    pallas_call x1, Pallas kernels, on_device(): pl.pallas_call(local_kernel, out_shape=[pltpu.VMEM((states, 2 * HEAD), jn...  3.41 us
  transfers between devices with their start and end apart: 25, of which 17 were waited for; matrix products, arithmetic and copies ran while one was open for 5% of the time, Pallas kernels for 22%

profile of v1, /device:TPU:0, one launch (start us, length us, event | category | flops | bytes accessed | tf_op | source)
XLA Modules:
  0.0 113.8 jit_solution(1161422203300627775)
XLA Ops:
  0.0 7.5 %all-to-all-start = ((bf16[16,8,512]{2,1,0:T(8,128)(2,1)}), bf16[16,8,512]{2,1,0:T(8,128)(2,1)S(1)}, u32[]{:S(2)}, u32[]{:S(2)}) async-start(bf16[16,8,512]{2,1,0:T(8,128)(2,1)} %bitcast.121), calls=%async_computation | async-start | bytes 262144 | tf_op jit(solution)/shard_map/all_to_all | solution.py:256
  10.0 3.4 %shard_map.145 = (bf16[1024,128]{1,0:T(8,128)(2,1)S(1)}, f32[1024,128]{1,0:T(8,128)S(1)}) custom-call(f32[16]{0:T(128)S(1)} %copy-done, bf16[64,1024]{1,0:T(8,128)(2,1)} %query_ref.1, bf16[64,512]{1,0:T(8,128)(2,1)} %kv_ref.1, bf16[256,512]{1,0:T(8,128)(2,1)} %local_ref.1, f32[64,128]{1,0:T(8,128)S(1)} %get-tuple-element.80.cos_ref, ...), custom_call_target="tpu_custom_call" | custom-call | tf_op jit(solution)/shard_map/pallas_call | solution.py:284
  14.2 1.2 %all-to-all-done = bf16[16,8,512]{2,1,0:T(8,128)(2,1)S(1)} async-done(((bf16[16,8,512]{2,1,0:T(8,128)(2,1)}), bf16[16,8,512]{2,1,0:T(8,128)(2,1)S(1)}, u32[]{:S(2)}, u32[]{:S(2)}) %all-to-all-start) | async-done | bytes 131104 | tf_op jit(solution)/shard_map/all_to_all | solution.py:256
  15.5 2.9 %shard_map.146 = (bf16[64,1024]{1,0:T(8,128)(2,1)S(1)}, bf16[64,1440]{1,0:T(8,128)(2,1)S(1)}) custom-call(s32[1]{0:T(128)} %bitcast.me_ref, bf16[2,1440,1024]{2,1,0:T(8,128)(2,1)} %bitcast.109, bf16[1024,128]{1,0:T(8,128)(2,1)S(1)} %get-tuple-element.31.rotated_ref, f32[1024,128]{1,0:T(8,128)S(1)} %get-tuple-element.32.state_ref, ...), custom_call_target="tpu_custom_call" | custom-call | tf_op jit(solution)/shard_map/pallas_call | solution.py:215
  18.4 1.6 %collective-permute-start = (bf16[64,1440]{1,0:T(8,128)(2,1)S(1)}, bf16[64,1440]{1,0:T(8,128)(2,1)S(1)}, u32[]{:S(2)}, u32[]{:S(2)}) collective-permute-start(bf16[64,1440]{1,0:T(8,128)(2,1)S(1)} %get-tuple-element.37), channel_id=1, source_target_pairs={{0,1},{1,0},{2,3},{3,2},{4,5},{5,4},{6,7},{7,6},{8,9},{9,8},{10,11... | collective-permute-start | bytes 552968 | tf_op jit(solution)/shard_map/ppermute | solution.py:24
  20.8 2.9 %shard_map.147 = (f32[64,1440]{1,0:T(8,128)S(1)}, bf16[64,1440]{1,0:T(8,128)(2,1)S(1)}) custom-call(s32[1]{0:T(128)} %bitcast.me_ref, bf16[2,1440,1024]{2,1,0:T(8,128)(2,1)} %bitcast.110, bf16[64,1440]{1,0:T(8,128)(2,1)} %residual_ref.1, bf16[64,1024]{1,0:T(8,128)(2,1)S(1)} %get-tuple-element.35.attended_ref), custom_call_target="tpu_custom_call" | custom-call | tf_op jit(solution)/shard_map/pallas_call | solution.py:215
  24.6 2.4 %collective-permute-start.4 = (bf16[64,1440]{1,0:T(8,128)(2,1)S(1)}, bf16[64,1440]{1,0:T(8,128)(2,1)S(1)}, u32[]{:S(2)}, u32[]{:S(2)}) collective-permute-start(bf16[64,1440]{1,0:T(8,128)(2,1)S(1)} %fusion.4), channel_id=1, source_target_pairs={{0,16},{2,18},{4,20},{6,22},{8,24},{10,26},{12,28},{14,30},{16,0},... | collective-permute-start | bytes 552968 | tf_op jit(solution)/shard_map/ppermute | solution.py:24
  27.1 1.5 %collective-permute-start.1 = (bf16[64,1440]{1,0:T(8,128)(2,1)S(1)}, bf16[64,1440]{1,0:T(8,128)(2,1)S(1)}, u32[]{:S(2)}, u32[]{:S(2)}) collective-permute-start(bf16[64,1440]{1,0:T(8,128)(2,1)S(1)} %get-tuple-element.40), channel_id=1, source_target_pairs={{0,1},{1,0},{2,3},{3,2},{4,5},{5,4},{6,7},{7,6},{8,9},{9,8},{10,11... | collective-permute-start | bytes 552968 | tf_op jit(solution)/shard_map/ppermute | solution.py:24
  28.8 4.1 %collective-permute-done.1 = bf16[64,1440]{1,0:T(8,128)(2,1)S(1)} collective-permute-done((bf16[64,1440]{1,0:T(8,128)(2,1)S(1)}, bf16[64,1440]{1,0:T(8,128)(2,1)S(1)}, u32[]{:S(2)}, u32[]{:S(2)}) %collective-permute-start.1) | collective-permute-done | bytes 184352 | tf_op jit(solution)/shard_map/ppermute | solution.py:24
  33.4 1.5 %collective-permute-start.3 = (bf16[2,40,1440]{2,1,0:T(8,128)(2,1)S(1)}, bf16[2,40,1440]{2,1,0:T(8,128)(2,1)S(1)}, u32[]{:S(2)}, u32[]{:S(2)}) collective-permute-start(bf16[2,40,1440]{2,1,0:T(8,128)(2,1)S(1)} %get-tuple-element.63), channel_id=1, source_target_pairs={{0,4},{2,6},{4,0},{6,2},{8,12},{10,14},{12,8},{14,10},{16,20},{18,... | collective-permute-start | bytes 691208 | tf_op jit(solution)/shard_map/ppermute | solution.py:24
  35.5 1.5 %collective-permute-start.7 = (bf16[2,40,1440]{2,1,0:T(8,128)(2,1)S(1)}, bf16[2,40,1440]{2,1,0:T(8,128)(2,1)S(1)}, u32[]{:S(2)}, u32[]{:S(2)}) collective-permute-start(bf16[2,40,1440]{2,1,0:T(8,128)(2,1)S(1)} %get-tuple-element.61), channel_id=1, source_target_pairs={{0,12},{2,14},{4,8},{6,10},{8,4},{10,6},{12,0},{14,2},{16,28},{18,... | collective-permute-start | bytes 691208 | tf_op jit(solution)/shard_map/ppermute | solution.py:24
  37.4 1.5 %collective-permute-start.5 = (bf16[64,1440]{1,0:T(8,128)(2,1)S(1)}, bf16[64,1440]{1,0:T(8,128)(2,1)S(1)}, u32[]{:S(2)}, u32[]{:S(2)}) collective-permute-start(bf16[64,1440]{1,0:T(8,128)(2,1)S(1)} %collective-permute-done.4), channel_id=1, source_target_pairs={{0,1},{1,0},{2,3},{3,2},{4,5},{5,4},{6,7},{7,6},{8,9},{9,8},{10,11... | collective-permute-start | bytes 552968 | tf_op jit(solution)/shard_map/ppermute | solution.py:24
  39.6 4.7 %collective-permute-done.3 = bf16[2,40,1440]{2,1,0:T(8,128)(2,1)S(1)} collective-permute-done((bf16[2,40,1440]{2,1,0:T(8,128)(2,1)S(1)}, bf16[2,40,1440]{2,1,0:T(8,128)(2,1)S(1)}, u32[]{:S(2)}, u32[]{:S(2)}) %collective-permute-start.3) | collective-permute-done | bytes 230432 | tf_op jit(solution)/shard_map/ppermute | solution.py:24
  45.1 1.2 %collective-permute-done.6 = bf16[2,40,1440]{2,1,0:T(8,128)(2,1)S(1)} collective-permute-done((bf16[2,40,1440]{2,1,0:T(8,128)(2,1)S(1)}, bf16[2,40,1440]{2,1,0:T(8,128)(2,1)S(1)}, u32[]{:S(2)}, u32[]{:S(2)}) %collective-permute-start.6) | collective-permute-done | bytes 230432 | tf_op jit(solution)/shard_map/ppermute | solution.py:24
  46.6 2.4 %collective-permute-start.11 = (bf16[2,40,1440]{2,1,0:T(8,128)(2,1)S(1)}, bf16[2,40,1440]{2,1,0:T(8,128)(2,1)S(1)}, u32[]{:S(2)}, u32[]{:S(2)}) collective-permute-start(bf16[2,40,1440]{2,1,0:T(8,128)(2,1)S(1)} %get-tuple-element.57), channel_id=1, source_target_pairs={{0,12},{2,14},{4,8},{6,10},{8,4},{10,6},{12,0},{14,2},{16,28},{18,... | collective-permute-start | bytes 691208 | tf_op jit(solution)/shard_map/ppermute | solution.py:24
  50.1 6.0 %shard_map.148.refs_0_ = bf16[320,720]{1,0:T(8,128)(2,1)S(1)} custom-call(s32[1]{0:T(128)} %bitcast.me_ref, bf16[3,240,2880]{2,1,0:T(8,128)(2,1)} %bitcast.113, bf16[3,240,2880]{2,1,0:T(8,128)(2,1)} %bitcast.115, f32[1,2880]{1,0:T(1,128)} %reshape.153.gain_ref, bf16[2,160,1440]{2,1,0:T(8,128)(2,1)S(1)} %constant_dynamic-update-slice_fusion.refs_0_, ...), custom_call_target="tpu_custom_call" | custom-call | tf_op jit(solution)/shard_map/pallas_call | solution.py:215
  56.3 5.2 %collective-permute-done.10 = bf16[2,40,1440]{2,1,0:T(8,128)(2,1)S(1)} collective-permute-done((bf16[2,40,1440]{2,1,0:T(8,128)(2,1)S(1)}, bf16[2,40,1440]{2,1,0:T(8,128)(2,1)S(1)}, u32[]{:S(2)}, u32[]{:S(2)}) %collective-permute-start.10) | collective-permute-done | bytes 230432 | tf_op jit(solution)/shard_map/ppermute | solution.py:24
  61.7 1.6 %collective-permute-start.13 = (bf16[320,720]{1,0:T(8,128)(2,1)S(1)}, bf16[320,720]{1,0:T(8,128)(2,1)S(1)}, u32[]{:S(2)}, u32[]{:S(2)}) collective-permute-start(bf16[320,720]{1,0:T(8,128)(2,1)S(1)} %shard_map.148.refs_0_), channel_id=1, source_target_pairs={{0,1},{1,0},{2,3},{3,2},{4,5},{5,4},{6,7},{7,6},{8,9},{9,8},{10,11... | collective-permute-start | bytes 1382408 | tf_op jit(solution)/shard_map/ppermute | solution.py:24
  64.3 6.2 %shard_map.149.refs_0_ = bf16[320,720]{1,0:T(8,128)(2,1)S(1)} custom-call(s32[1]{0:T(128)} %bitcast.me_ref, bf16[3,240,2880]{2,1,0:T(8,128)(2,1)} %bitcast.114, bf16[3,240,2880]{2,1,0:T(8,128)(2,1)} %bitcast.116, f32[1,2880]{1,0:T(1,128)} %reshape.153.gain_ref, bf16[2,160,1440]{2,1,0:T(8,128)(2,1)S(1)} %constant_dynamic-update-slice_fusion.4.refs_0_, ...), custom_call_target="tpu_custom_call" | custom-call | tf_op jit(solution)/shard_map/pallas_call | solution.py:215
  70.5 1.6 %collective-permute-start.18 = (bf16[320,720]{1,0:T(8,128)(2,1)S(1)}, bf16[320,720]{1,0:T(8,128)(2,1)S(1)}, u32[]{:S(2)}, u32[]{:S(2)}) collective-permute-start(bf16[320,720]{1,0:T(8,128)(2,1)S(1)} %shard_map.149.refs_0_), channel_id=1, source_target_pairs={{0,1},{1,0},{2,3},{3,2},{4,5},{5,4},{6,7},{7,6},{8,9},{9,8},{10,11... | collective-permute-start | bytes 1382408 | tf_op jit(solution)/shard_map/ppermute | solution.py:24
  72.0 3.8 %collective-permute-done.13.refs_1_ = bf16[320,720]{1,0:T(8,128)(2,1)S(1)} collective-permute-done((bf16[320,720]{1,0:T(8,128)(2,1)S(1)}, bf16[320,720]{1,0:T(8,128)(2,1)S(1)}, u32[]{:S(2)}, u32[]{:S(2)}) %collective-permute-start.13) | collective-permute-done | bytes 460832 | tf_op jit(solution)/shard_map/ppermute | solution.py:24
  75.8 3.5 %shard_map.150 = (bf16[160,1440]{1,0:T(8,128)(2,1)S(1)}, bf16[160,1440]{1,0:T(8,128)(2,1)S(1)}) custom-call(s32[1]{0:T(128)} %bitcast.me_ref, bf16[2,720,1440]{2,1,0:T(8,128)(2,1)} %bitcast.111, bf16[320,720]{1,0:T(8,128)(2,1)S(1)} %shard_map.148.refs_0_, bf16[320,720]{1,0:T(8,128)(2,1)S(1)} %collective-permute-done.13.refs_1_), custom_call_target="tpu_custom_call" | custom-call | tf_op jit(solution)/shard_map/pallas_call | solution.py:215
  79.6 6.2 %collective-permute-done.18.refs_1_ = bf16[320,720]{1,0:T(8,128)(2,1)S(1)} collective-permute-done((bf16[320,720]{1,0:T(8,128)(2,1)S(1)}, bf16[320,720]{1,0:T(8,128)(2,1)S(1)}, u32[]{:S(2)}, u32[]{:S(2)}) %collective-permute-start.18) | collective-permute-done | bytes 460832 | tf_op jit(solution)/shard_map/ppermute | solution.py:24
  85.9 3.5 %shard_map.151 = (bf16[160,1440]{1,0:T(8,128)(2,1)S(1)}, bf16[160,1440]{1,0:T(8,128)(2,1)S(1)}) custom-call(s32[1]{0:T(128)} %bitcast.me_ref, bf16[2,720,1440]{2,1,0:T(8,128)(2,1)} %bitcast.112, bf16[320,720]{1,0:T(8,128)(2,1)S(1)} %shard_map.149.refs_0_, bf16[320,720]{1,0:T(8,128)(2,1)S(1)} %collective-permute-done.18.refs_1_), custom_call_target="tpu_custom_call" | custom-call | tf_op jit(solution)/shard_map/pallas_call | solution.py:215
  89.6 1.7 %collective-permute-done.19 = bf16[160,1440]{1,0:T(8,128)(2,1)S(1)} collective-permute-done((bf16[160,1440]{1,0:T(8,128)(2,1)S(1)}, bf16[160,1440]{1,0:T(8,128)(2,1)S(1)}, u32[]{:S(2)}, u32[]{:S(2)}) %collective-permute-start.19) | collective-permute-done | bytes 460832 | tf_op jit(solution)/shard_map/ppermute | solution.py:24
  91.5 1.5 %collective-permute-start.20 = (bf16[40,1440]{1,0:T(8,128)(2,1)S(1)}, bf16[40,1440]{1,0:T(8,128)(2,1)S(1)}, u32[]{:S(2)}, u32[]{:S(2)}) collective-permute-start(bf16[40,1440]{1,0:T(8,128)(2,1)S(1)} %get-tuple-element.68), channel_id=1, source_target_pairs={{0,4},{2,6},{4,0},{6,2},{8,12},{10,14},{12,8},{14,10},{16,20},{18,... | collective-permute-start | bytes 345608 | tf_op jit(solution)/shard_map/ppermute | solution.py:24
  95.1 1.5 %collective-permute-start.15 = (bf16[40,1440]{1,0:T(8,128)(2,1)S(1)}, bf16[40,1440]{1,0:T(8,128)(2,1)S(1)}, u32[]{:S(2)}, u32[]{:S(2)}) collective-permute-start(bf16[40,1440]{1,0:T(8,128)(2,1)S(1)} %get-tuple-element.72), channel_id=1, source_target_pairs={{0,4},{2,6},{4,0},{6,2},{8,12},{10,14},{12,8},{14,10},{16,20},{18,... | collective-permute-start | bytes 345608 | tf_op jit(solution)/shard_map/ppermute | solution.py:24
  99.2 2.6 %collective-permute-done.22 = bf16[40,1440]{1,0:T(8,128)(2,1)S(1)} collective-permute-done((bf16[40,1440]{1,0:T(8,128)(2,1)S(1)}, bf16[40,1440]{1,0:T(8,128)(2,1)S(1)}, u32[]{:S(2)}, u32[]{:S(2)}) %collective-permute-start.22) | collective-permute-done | bytes 115232 | tf_op jit(solution)/shard_map/ppermute | solution.py:24
  102.2 2.3 %collective-permute-start.23 = (bf16[64,1440]{1,0:T(8,128)(2,1)S(1)}, bf16[64,1440]{1,0:T(8,128)(2,1)S(1)}, u32[]{:S(2)}, u32[]{:S(2)}) collective-permute-start(bf16[64,1440]{1,0:T(8,128)(2,1)S(1)} %fusion.3), channel_id=1, source_target_pairs={{0,16},{2,18},{4,20},{6,22},{8,24},{10,26},{12,28},{14,30},{16,0},... | collective-permute-start | bytes 552968 | tf_op jit(solution)/shard_map/ppermute | solution.py:24
  104.5 2.0 %collective-permute-done.16 = bf16[40,1440]{1,0:T(8,128)(2,1)S(1)} collective-permute-done((bf16[40,1440]{1,0:T(8,128)(2,1)S(1)}, bf16[40,1440]{1,0:T(8,128)(2,1)S(1)}, u32[]{:S(2)}, u32[]{:S(2)}) %collective-permute-start.16) | collective-permute-done | bytes 115232 | tf_op jit(solution)/shard_map/ppermute | solution.py:24
  106.5 1.9 %collective-permute-done.17 = bf16[40,1440]{1,0:T(8,128)(2,1)S(1)} collective-permute-done((bf16[40,1440]{1,0:T(8,128)(2,1)S(1)}, bf16[40,1440]{1,0:T(8,128)(2,1)S(1)}, u32[]{:S(2)}, u32[]{:S(2)}) %collective-permute-start.17) | collective-permute-done | bytes 115232 | tf_op jit(solution)/shard_map/ppermute | solution.py:24
  108.7 4.2 %collective-permute-done.23 = bf16[64,1440]{1,0:T(8,128)(2,1)S(1)} collective-permute-done((bf16[64,1440]{1,0:T(8,128)(2,1)S(1)}, bf16[64,1440]{1,0:T(8,128)(2,1)S(1)}, u32[]{:S(2)}, u32[]{:S(2)}) %collective-permute-start.23) | collective-permute-done | bytes 184352 | tf_op jit(solution)/shard_map/ppermute | solution.py:24
  (80 shorter events, 17.3 us)
Async XLA Ops:
  0.0 20.2 %copy-start.1 = (f32[2880]{0:T(1024)S(1)}, f32[2880]{0:T(1024)}, u32[]{:S(2)}) copy-start(f32[2880]{0:T(1024)} %param.24) | copy-start | bytes 34564
  0.0 15.5 %all-to-all-start = ((bf16[16,8,512]{2,1,0:T(8,128)(2,1)}), bf16[16,8,512]{2,1,0:T(8,128)(2,1)S(1)}, u32[]{:S(2)}, u32[]{:S(2)}) async-start(bf16[16,8,512]{2,1,0:T(8,128)(2,1)} %bitcast.121), calls=%async_computation | async-start | bytes 262144 | tf_op jit(solution)/shard_map/all_to_all | solution.py:256
  9.4 0.7 copy-start
  18.4 5.3 %copy-start.2 = (f32[64,4]{0,1:T(4,128)S(1)}, f32[64,4]{0,1:T(4,128)}, u32[]{:S(2)}) copy-start(f32[64,4]{0,1:T(4,128)} %param.26) | copy-start | bytes 3076
  18.4 6.2 %collective-permute-start = (bf16[64,1440]{1,0:T(8,128)(2,1)S(1)}, bf16[64,1440]{1,0:T(8,128)(2,1)S(1)}, u32[]{:S(2)}, u32[]{:S(2)}) collective-permute-start(bf16[64,1440]{1,0:T(8,128)(2,1)S(1)} %get-tuple-element.37), channel_id=1, source_target_pairs={{0,1},{1,0},{2,3},{3,2},{4,5},{5,4},{6,7},{7,6},{8,9},{9,8},{10,11... | collective-permute-start | bytes 552968 | tf_op jit(solution)/shard_map/ppermute | solution.py:24
  24.6 12.7 %collective-permute-start.4 = (bf16[64,1440]{1,0:T(8,128)(2,1)S(1)}, bf16[64,1440]{1,0:T(8,128)(2,1)S(1)}, u32[]{:S(2)}, u32[]{:S(2)}) collective-permute-start(bf16[64,1440]{1,0:T(8,128)(2,1)S(1)} %fusion.4), channel_id=1, source_target_pairs={{0,16},{2,18},{4,20},{6,22},{8,24},{10,26},{12,28},{14,30},{16,0},... | collective-permute-start | bytes 552968 | tf_op jit(solution)/shard_map/ppermute | solution.py:24
  27.1 5.8 %collective-permute-start.1 = (bf16[64,1440]{1,0:T(8,128)(2,1)S(1)}, bf16[64,1440]{1,0:T(8,128)(2,1)S(1)}, u32[]{:S(2)}, u32[]{:S(2)}) collective-permute-start(bf16[64,1440]{1,0:T(8,128)(2,1)S(1)} %get-tuple-element.40), channel_id=1, source_target_pairs={{0,1},{1,0},{2,3},{3,2},{4,5},{5,4},{6,7},{7,6},{8,9},{9,8},{10,11... | collective-permute-start | bytes 552968 | tf_op jit(solution)/shard_map/ppermute | solution.py:24
  33.4 10.9 %collective-permute-start.3 = (bf16[2,40,1440]{2,1,0:T(8,128)(2,1)S(1)}, bf16[2,40,1440]{2,1,0:T(8,128)(2,1)S(1)}, u32[]{:S(2)}, u32[]{:S(2)}) collective-permute-start(bf16[2,40,1440]{2,1,0:T(8,128)(2,1)S(1)} %get-tuple-element.63), channel_id=1, source_target_pairs={{0,4},{2,6},{4,0},{6,2},{8,12},{10,14},{12,8},{14,10},{16,20},{18,... | collective-permute-start | bytes 691208 | tf_op jit(solution)/shard_map/ppermute | solution.py:24
  34.9 4.7 %collective-permute-start.2 = (f32[64,8]{0,1:T(8,128)S(1)}, f32[64,8]{0,1:T(8,128)S(1)}, u32[]{:S(2)}, u32[]{:S(2)}) collective-permute-start(f32[64,8]{0,1:T(8,128)S(1)} %pad_maximum_fusion.8), channel_id=1, source_target_pairs={{0,16},{2,18},{4,20},{6,22},{8,24},{10,26},{12,28},{14,30},{16,0},... | collective-permute-start | bytes 6152 | tf_op jit(solution)/shard_map/ppermute | solution.py:24
  35.5 9.6 %collective-permute-start.7 = (bf16[2,40,1440]{2,1,0:T(8,128)(2,1)S(1)}, bf16[2,40,1440]{2,1,0:T(8,128)(2,1)S(1)}, u32[]{:S(2)}, u32[]{:S(2)}) collective-permute-start(bf16[2,40,1440]{2,1,0:T(8,128)(2,1)S(1)} %get-tuple-element.61), channel_id=1, source_target_pairs={{0,12},{2,14},{4,8},{6,10},{8,4},{10,6},{12,0},{14,2},{16,28},{18,... | collective-permute-start | bytes 691208 | tf_op jit(solution)/shard_map/ppermute | solution.py:24
  37.0 9.3 %collective-permute-start.6 = (bf16[2,40,1440]{2,1,0:T(8,128)(2,1)S(1)}, bf16[2,40,1440]{2,1,0:T(8,128)(2,1)S(1)}, u32[]{:S(2)}, u32[]{:S(2)}) collective-permute-start(bf16[2,40,1440]{2,1,0:T(8,128)(2,1)S(1)} %get-tuple-element.64), channel_id=1, source_target_pairs={{0,8},{2,10},{4,12},{6,14},{8,0},{10,2},{12,4},{14,6},{16,24},{18,... | collective-permute-start | bytes 691208 | tf_op jit(solution)/shard_map/ppermute | solution.py:24
  37.4 7.5 %collective-permute-start.5 = (bf16[64,1440]{1,0:T(8,128)(2,1)S(1)}, bf16[64,1440]{1,0:T(8,128)(2,1)S(1)}, u32[]{:S(2)}, u32[]{:S(2)}) collective-permute-start(bf16[64,1440]{1,0:T(8,128)(2,1)S(1)} %collective-permute-done.4), channel_id=1, source_target_pairs={{0,1},{1,0},{2,3},{3,2},{4,5},{5,4},{6,7},{7,6},{8,9},{9,8},{10,11... | collective-permute-start | bytes 552968 | tf_op jit(solution)/shard_map/ppermute | solution.py:24
  46.4 3.7 %collective-permute-start.8 = (bf16[2,160,1440]{2,1,0:T(8,128)(2,1)S(1)}, bf16[2,160,1440]{2,1,0:T(8,128)(2,1)S(1)}, u32[]{:S(2)}, u32[]{:S(2)}) collective-permute-start(bf16[2,160,1440]{2,1,0:T(8,128)(2,1)S(1)} %constant_dynamic-update-slice_fusion.refs_0_), channel_id=1, source_target_pairs={{0,2},{2,0},{4,6},{6,4},{8,10},{10,8},{12,14},{14,12},{16,18},{18,... | collective-permute-start | bytes 2764808 | tf_op jit(solution)/shard_map/ppermute | solution.py:24
  46.6 9.8 %collective-permute-start.11 = (bf16[2,40,1440]{2,1,0:T(8,128)(2,1)S(1)}, bf16[2,40,1440]{2,1,0:T(8,128)(2,1)S(1)}, u32[]{:S(2)}, u32[]{:S(2)}) collective-permute-start(bf16[2,40,1440]{2,1,0:T(8,128)(2,1)S(1)} %get-tuple-element.57), channel_id=1, source_target_pairs={{0,12},{2,14},{4,8},{6,10},{8,4},{10,6},{12,0},{14,2},{16,28},{18,... | collective-permute-start | bytes 691208 | tf_op jit(solution)/shard_map/ppermute | solution.py:24
  49.0 12.6 %collective-permute-start.10 = (bf16[2,40,1440]{2,1,0:T(8,128)(2,1)S(1)}, bf16[2,40,1440]{2,1,0:T(8,128)(2,1)S(1)}, u32[]{:S(2)}, u32[]{:S(2)}) collective-permute-start(bf16[2,40,1440]{2,1,0:T(8,128)(2,1)S(1)} %get-tuple-element.60), channel_id=1, source_target_pairs={{0,8},{2,10},{4,12},{6,14},{8,0},{10,2},{12,4},{14,6},{16,24},{18,... | collective-permute-start | bytes 691208 | tf_op jit(solution)/shard_map/ppermute | solution.py:24
  49.9 11.6 %collective-permute-start.9 = (bf16[2,40,1440]{2,1,0:T(8,128)(2,1)S(1)}, bf16[2,40,1440]{2,1,0:T(8,128)(2,1)S(1)}, u32[]{:S(2)}, u32[]{:S(2)}) collective-permute-start(bf16[2,40,1440]{2,1,0:T(8,128)(2,1)S(1)} %get-tuple-element.59), channel_id=1, source_target_pairs={{0,4},{2,6},{4,0},{6,2},{8,12},{10,14},{12,8},{14,10},{16,20},{18,... | collective-permute-start | bytes 691208 | tf_op jit(solution)/shard_map/ppermute | solution.py:24
  61.6 2.6 %collective-permute-start.12 = (bf16[2,160,1440]{2,1,0:T(8,128)(2,1)S(1)}, bf16[2,160,1440]{2,1,0:T(8,128)(2,1)S(1)}, u32[]{:S(2)}, u32[]{:S(2)}) collective-permute-start(bf16[2,160,1440]{2,1,0:T(8,128)(2,1)S(1)} %constant_dynamic-update-slice_fusion.4.refs_0_), channel_id=1, source_target_pairs={{0,2},{2,0},{4,6},{6,4},{8,10},{10,8},{12,14},{14,12},{16,18},{18,... | collective-permute-start | bytes 2764808 | tf_op jit(solution)/shard_map/ppermute | solution.py:24
  61.7 14.1 %collective-permute-start.13 = (bf16[320,720]{1,0:T(8,128)(2,1)S(1)}, bf16[320,720]{1,0:T(8,128)(2,1)S(1)}, u32[]{:S(2)}, u32[]{:S(2)}) collective-permute-start(bf16[320,720]{1,0:T(8,128)(2,1)S(1)} %shard_map.148.refs_0_), channel_id=1, source_target_pairs={{0,1},{1,0},{2,3},{3,2},{4,5},{5,4},{6,7},{7,6},{8,9},{9,8},{10,11... | collective-permute-start | bytes 1382408 | tf_op jit(solution)/shard_map/ppermute | solution.py:24
  70.5 15.4 %collective-permute-start.18 = (bf16[320,720]{1,0:T(8,128)(2,1)S(1)}, bf16[320,720]{1,0:T(8,128)(2,1)S(1)}, u32[]{:S(2)}, u32[]{:S(2)}) collective-permute-start(bf16[320,720]{1,0:T(8,128)(2,1)S(1)} %shard_map.149.refs_0_), channel_id=1, source_target_pairs={{0,1},{1,0},{2,3},{3,2},{4,5},{5,4},{6,7},{7,6},{8,9},{9,8},{10,11... | collective-permute-start | bytes 1382408 | tf_op jit(solution)/shard_map/ppermute | solution.py:24
  79.3 10.2 %collective-permute-start.14 = (bf16[160,1440]{1,0:T(8,128)(2,1)S(1)}, bf16[160,1440]{1,0:T(8,128)(2,1)S(1)}, u32[]{:S(2)}, u32[]{:S(2)}) collective-permute-start(bf16[160,1440]{1,0:T(8,128)(2,1)S(1)} %get-tuple-element.53), channel_id=1, source_target_pairs={{0,2},{2,0},{4,6},{6,4},{8,10},{10,8},{12,14},{14,12},{16,18},{18,... | collective-permute-start | bytes 1382408 | tf_op jit(solution)/shard_map/ppermute | solution.py:24
  89.4 1.9 %collective-permute-start.19 = (bf16[160,1440]{1,0:T(8,128)(2,1)S(1)}, bf16[160,1440]{1,0:T(8,128)(2,1)S(1)}, u32[]{:S(2)}, u32[]{:S(2)}) collective-permute-start(bf16[160,1440]{1,0:T(8,128)(2,1)S(1)} %get-tuple-element.56), channel_id=1, source_target_pairs={{0,2},{2,0},{4,6},{6,4},{8,10},{10,8},{12,14},{14,12},{16,18},{18,... | collective-permute-start | bytes 1382408 | tf_op jit(solution)/shard_map/ppermute | solution.py:24
  91.5 6.2 %collective-permute-start.20 = (bf16[40,1440]{1,0:T(8,128)(2,1)S(1)}, bf16[40,1440]{1,0:T(8,128)(2,1)S(1)}, u32[]{:S(2)}, u32[]{:S(2)}) collective-permute-start(bf16[40,1440]{1,0:T(8,128)(2,1)S(1)} %get-tuple-element.68), channel_id=1, source_target_pairs={{0,4},{2,6},{4,0},{6,2},{8,12},{10,14},{12,8},{14,10},{16,20},{18,... | collective-permute-start | bytes 345608 | tf_op jit(solution)/shard_map/ppermute | solution.py:24
  92.9 6.2 %collective-permute-start.21 = (bf16[40,1440]{1,0:T(8,128)(2,1)S(1)}, bf16[40,1440]{1,0:T(8,128)(2,1)S(1)}, u32[]{:S(2)}, u32[]{:S(2)}) collective-permute-start(bf16[40,1440]{1,0:T(8,128)(2,1)S(1)} %get-tuple-element.67), channel_id=1, source_target_pairs={{0,8},{2,10},{4,12},{6,14},{8,0},{10,2},{12,4},{14,6},{16,24},{18,... | collective-permute-start | bytes 345608 | tf_op jit(solution)/shard_map/ppermute | solution.py:24
  94.1 7.7 %collective-permute-start.22 = (bf16[40,1440]{1,0:T(8,128)(2,1)S(1)}, bf16[40,1440]{1,0:T(8,128)(2,1)S(1)}, u32[]{:S(2)}, u32[]{:S(2)}) collective-permute-start(bf16[40,1440]{1,0:T(8,128)(2,1)S(1)} %get-tuple-element.66), channel_id=1, source_target_pairs={{0,12},{2,14},{4,8},{6,10},{8,4},{10,6},{12,0},{14,2},{16,28},{18,... | collective-permute-start | bytes 345608 | tf_op jit(solution)/shard_map/ppermute | solution.py:24
  95.1 9.5 %collective-permute-start.15 = (bf16[40,1440]{1,0:T(8,128)(2,1)S(1)}, bf16[40,1440]{1,0:T(8,128)(2,1)S(1)}, u32[]{:S(2)}, u32[]{:S(2)}) collective-permute-start(bf16[40,1440]{1,0:T(8,128)(2,1)S(1)} %get-tuple-element.72), channel_id=1, source_target_pairs={{0,4},{2,6},{4,0},{6,2},{8,12},{10,14},{12,8},{14,10},{16,20},{18,... | collective-permute-start | bytes 345608 | tf_op jit(solution)/shard_map/ppermute | solution.py:24
  96.5 10.0 %collective-permute-start.16 = (bf16[40,1440]{1,0:T(8,128)(2,1)S(1)}, bf16[40,1440]{1,0:T(8,128)(2,1)S(1)}, u32[]{:S(2)}, u32[]{:S(2)}) collective-permute-start(bf16[40,1440]{1,0:T(8,128)(2,1)S(1)} %get-tuple-element.71), channel_id=1, source_target_pairs={{0,8},{2,10},{4,12},{6,14},{8,0},{10,2},{12,4},{14,6},{16,24},{18,... | collective-permute-start | bytes 345608 | tf_op jit(solution)/shard_map/ppermute | solution.py:24
  97.6 10.8 %collective-permute-start.17 = (bf16[40,1440]{1,0:T(8,128)(2,1)S(1)}, bf16[40,1440]{1,0:T(8,128)(2,1)S(1)}, u32[]{:S(2)}, u32[]{:S(2)}) collective-permute-start(bf16[40,1440]{1,0:T(8,128)(2,1)S(1)} %get-tuple-element.70), channel_id=1, source_target_pairs={{0,12},{2,14},{4,8},{6,10},{8,4},{10,6},{12,0},{14,2},{16,28},{18,... | collective-permute-start | bytes 345608 | tf_op jit(solution)/shard_map/ppermute | solution.py:24
  102.2 10.7 %collective-permute-start.23 = (bf16[64,1440]{1,0:T(8,128)(2,1)S(1)}, bf16[64,1440]{1,0:T(8,128)(2,1)S(1)}, u32[]{:S(2)}, u32[]{:S(2)}) collective-permute-start(bf16[64,1440]{1,0:T(8,128)(2,1)S(1)} %fusion.3), channel_id=1, source_target_pairs={{0,16},{2,18},{4,20},{6,22},{8,24},{10,26},{12,28},{14,30},{16,0},... | collective-permute-start | bytes 552968 | tf_op jit(solution)/shard_map/ppermute | solution.py:24

commit v2 on v1

--- a/solution.py
+++ b/solution.py
@@ -423,7 +423,7 @@
     far_blocks = whole(exchange(state_sent, "group", experts))
     own_sent = picked(own_pick, own_blocks)
     own_pieces = send_rows(own_sent)
-    far_plan = after(far_plan, own_pieces[1])
+    far_plan = after(far_plan, own_pieces[half // 2])
     far_pick, far_spread = slots(
         far_plan[:, :top_count].astype(jnp.int32), far_plan[:, top_count:]
     )

time: 114 us -> 116 us (1.018)
  waiting for transfers between devices: 41.9 us -> 44.7 us
  starting transfers between devices: 35.1 us -> 33.7 us
    ppermute x24, waiting for transfers between devices: 40.7 us -> 43.5 us  [exchange(): return lax.ppermute(value, axis, [(i, i ^ offset) for i in range(size)])]
    ppermute x24, starting transfers between devices: 27.6 us -> 26.2 us  [exchange(): return lax.ppermute(value, axis, [(i, i ^ offset) for i in range(size)])]
  transfers between devices with their start and end apart: 25 -> 25, of which waited for: 17 -> 19; matrix products, arithmetic and copies ran while one was open for 5% -> 5% of each run, Pallas kernels for 22% -> 22%
where the time goes in v2:
time: 116 us; the launch traced here: 115 us
  waiting for transfers between devices  44.7 us (39%)
  starting transfers between devices  33.7 us (29%)
  Pallas kernels  28.4 us (24%)
  matrix products  2.96 us (3%)
  other arithmetic  2.73 us (2%)
  local copies, waits for them, and re-layouts  1.66 us (1%)
    ppermute x24, waiting for transfers between devices, exchange(): return lax.ppermute(value, axis, [(i, i ^ offset) for i in range(size)])  43.5 us
    ppermute x24, starting transfers between devices, exchange(): return lax.ppermute(value, axis, [(i, i ^ offset) for i in range(size)])  26.2 us
    pallas_call x6, Pallas kernels, kernel_call(): pl.pallas_call(kernel, out_shape=[pltpu.VMEM(shape, dtype) for shape, dty...  25 us
    all_to_all x1, starting transfers between devices, on_device(): lax.all_to_all(remote_pool.reshape(groups, -1, lane_count), 'group', spli...  7.52 us
    pallas_call x1, Pallas kernels, on_device(): pl.pallas_call(local_kernel, out_shape=[pltpu.VMEM((states, 2 * HEAD), jn...  3.41 us
  transfers between devices with their start and end apart: 25, of which 19 were waited for; matrix products, arithmetic and copies ran while one was open for 5% of the time, Pallas kernels for 22%

profile of v2, /device:TPU:0, one launch (start us, length us, event | category | flops | bytes accessed | tf_op | source)
XLA Modules:
  0.0 115.3 jit_solution(868181885277082952)
XLA Ops:
  0.0 7.5 %all-to-all-start = ((bf16[16,8,512]{2,1,0:T(8,128)(2,1)}), bf16[16,8,512]{2,1,0:T(8,128)(2,1)S(1)}, u32[]{:S(2)}, u32[]{:S(2)}) async-start(bf16[16,8,512]{2,1,0:T(8,128)(2,1)} %bitcast.121), calls=%async_computation | async-start | bytes 262144 | tf_op jit(solution)/shard_map/all_to_all | solution.py:256
  10.0 3.4 %shard_map.145 = (bf16[1024,128]{1,0:T(8,128)(2,1)S(1)}, f32[1024,128]{1,0:T(8,128)S(1)}) custom-call(f32[16]{0:T(128)S(1)} %copy-done, bf16[64,1024]{1,0:T(8,128)(2,1)} %query_ref.1, bf16[64,512]{1,0:T(8,128)(2,1)} %kv_ref.1, bf16[256,512]{1,0:T(8,128)(2,1)} %local_ref.1, f32[64,128]{1,0:T(8,128)S(1)} %get-tuple-element.80.cos_ref, ...), custom_call_target="tpu_custom_call" | custom-call | tf_op jit(solution)/shard_map/pallas_call | solution.py:284
  15.5 2.9 %shard_map.146 = (bf16[64,1024]{1,0:T(8,128)(2,1)S(1)}, bf16[64,1440]{1,0:T(8,128)(2,1)S(1)}) custom-call(s32[1]{0:T(128)} %bitcast.me_ref, bf16[2,1440,1024]{2,1,0:T(8,128)(2,1)} %bitcast.109, bf16[1024,128]{1,0:T(8,128)(2,1)S(1)} %get-tuple-element.31.rotated_ref, f32[1024,128]{1,0:T(8,128)S(1)} %get-tuple-element.32.state_ref, ...), custom_call_target="tpu_custom_call" | custom-call | tf_op jit(solution)/shard_map/pallas_call | solution.py:215
  18.4 1.6 %collective-permute-start = (bf16[64,1440]{1,0:T(8,128)(2,1)S(1)}, bf16[64,1440]{1,0:T(8,128)(2,1)S(1)}, u32[]{:S(2)}, u32[]{:S(2)}) collective-permute-start(bf16[64,1440]{1,0:T(8,128)(2,1)S(1)} %get-tuple-element.37), channel_id=1, source_target_pairs={{0,1},{1,0},{2,3},{3,2},{4,5},{5,4},{6,7},{7,6},{8,9},{9,8},{10,11... | collective-permute-start | bytes 552968 | tf_op jit(solution)/shard_map/ppermute | solution.py:24
  20.8 2.9 %shard_map.147 = (f32[64,1440]{1,0:T(8,128)S(1)}, bf16[64,1440]{1,0:T(8,128)(2,1)S(1)}) custom-call(s32[1]{0:T(128)} %bitcast.me_ref, bf16[2,1440,1024]{2,1,0:T(8,128)(2,1)} %bitcast.110, bf16[64,1440]{1,0:T(8,128)(2,1)} %residual_ref.1, bf16[64,1024]{1,0:T(8,128)(2,1)S(1)} %get-tuple-element.35.attended_ref), custom_call_target="tpu_custom_call" | custom-call | tf_op jit(solution)/shard_map/pallas_call | solution.py:215
  24.6 2.4 %collective-permute-start.4 = (bf16[64,1440]{1,0:T(8,128)(2,1)S(1)}, bf16[64,1440]{1,0:T(8,128)(2,1)S(1)}, u32[]{:S(2)}, u32[]{:S(2)}) collective-permute-start(bf16[64,1440]{1,0:T(8,128)(2,1)S(1)} %fusion.4), channel_id=1, source_target_pairs={{0,16},{2,18},{4,20},{6,22},{8,24},{10,26},{12,28},{14,30},{16,0},... | collective-permute-start | bytes 552968 | tf_op jit(solution)/shard_map/ppermute | solution.py:24
  27.1 1.5 %collective-permute-start.1 = (bf16[64,1440]{1,0:T(8,128)(2,1)S(1)}, bf16[64,1440]{1,0:T(8,128)(2,1)S(1)}, u32[]{:S(2)}, u32[]{:S(2)}) collective-permute-start(bf16[64,1440]{1,0:T(8,128)(2,1)S(1)} %get-tuple-element.40), channel_id=1, source_target_pairs={{0,1},{1,0},{2,3},{3,2},{4,5},{5,4},{6,7},{7,6},{8,9},{9,8},{10,11... | collective-permute-start | bytes 552968 | tf_op jit(solution)/shard_map/ppermute | solution.py:24
  28.8 4.1 %collective-permute-done.1 = bf16[64,1440]{1,0:T(8,128)(2,1)S(1)} collective-permute-done((bf16[64,1440]{1,0:T(8,128)(2,1)S(1)}, bf16[64,1440]{1,0:T(8,128)(2,1)S(1)}, u32[]{:S(2)}, u32[]{:S(2)}) %collective-permute-start.1) | collective-permute-done | bytes 184352 | tf_op jit(solution)/shard_map/ppermute | solution.py:24
  33.4 1.5 %collective-permute-start.3 = (bf16[2,40,1440]{2,1,0:T(8,128)(2,1)S(1)}, bf16[2,40,1440]{2,1,0:T(8,128)(2,1)S(1)}, u32[]{:S(2)}, u32[]{:S(2)}) collective-permute-start(bf16[2,40,1440]{2,1,0:T(8,128)(2,1)S(1)} %get-tuple-element.63), channel_id=1, source_target_pairs={{0,8},{2,10},{4,12},{6,14},{8,0},{10,2},{12,4},{14,6},{16,24},{18,... | collective-permute-start | bytes 691208 | tf_op jit(solution)/shard_map/ppermute | solution.py:24
  35.5 1.5 %collective-permute-start.7 = (bf16[2,40,1440]{2,1,0:T(8,128)(2,1)S(1)}, bf16[2,40,1440]{2,1,0:T(8,128)(2,1)S(1)}, u32[]{:S(2)}, u32[]{:S(2)}) collective-permute-start(bf16[2,40,1440]{2,1,0:T(8,128)(2,1)S(1)} %get-tuple-element.61), channel_id=1, source_target_pairs={{0,12},{2,14},{4,8},{6,10},{8,4},{10,6},{12,0},{14,2},{16,28},{18,... | collective-permute-start | bytes 691208 | tf_op jit(solution)/shard_map/ppermute | solution.py:24
  37.4 1.5 %collective-permute-start.5 = (bf16[64,1440]{1,0:T(8,128)(2,1)S(1)}, bf16[64,1440]{1,0:T(8,128)(2,1)S(1)}, u32[]{:S(2)}, u32[]{:S(2)}) collective-permute-start(bf16[64,1440]{1,0:T(8,128)(2,1)S(1)} %collective-permute-done.4), channel_id=1, source_target_pairs={{0,1},{1,0},{2,3},{3,2},{4,5},{5,4},{6,7},{7,6},{8,9},{9,8},{10,11... | collective-permute-start | bytes 552968 | tf_op jit(solution)/shard_map/ppermute | solution.py:24
  38.8 2.2 %collective-permute-done.2 = f32[64,8]{0,1:T(8,128)S(1)} collective-permute-done((f32[64,8]{0,1:T(8,128)S(1)}, f32[64,8]{0,1:T(8,128)S(1)}, u32[]{:S(2)}, u32[]{:S(2)}) %collective-permute-start.2) | collective-permute-done | bytes 2080 | tf_op jit(solution)/shard_map/ppermute | solution.py:24
  41.1 1.3 %collective-permute-done.3 = bf16[2,40,1440]{2,1,0:T(8,128)(2,1)S(1)} collective-permute-done((bf16[2,40,1440]{2,1,0:T(8,128)(2,1)S(1)}, bf16[2,40,1440]{2,1,0:T(8,128)(2,1)S(1)}, u32[]{:S(2)}, u32[]{:S(2)}) %collective-permute-start.3) | collective-permute-done | bytes 230432 | tf_op jit(solution)/shard_map/ppermute | solution.py:24
  43.3 4.3 %collective-permute-done.7 = bf16[2,40,1440]{2,1,0:T(8,128)(2,1)S(1)} collective-permute-done((bf16[2,40,1440]{2,1,0:T(8,128)(2,1)S(1)}, bf16[2,40,1440]{2,1,0:T(8,128)(2,1)S(1)}, u32[]{:S(2)}, u32[]{:S(2)}) %collective-permute-start.7) | collective-permute-done | bytes 230432 | tf_op jit(solution)/shard_map/ppermute | solution.py:24
  49.2 1.4 %collective-permute-start.10 = (bf16[2,40,1440]{2,1,0:T(8,128)(2,1)S(1)}, bf16[2,40,1440]{2,1,0:T(8,128)(2,1)S(1)}, u32[]{:S(2)}, u32[]{:S(2)}) collective-permute-start(bf16[2,40,1440]{2,1,0:T(8,128)(2,1)S(1)} %get-tuple-element.60), channel_id=1, source_target_pairs={{0,8},{2,10},{4,12},{6,14},{8,0},{10,2},{12,4},{14,6},{16,24},{18,... | collective-permute-start | bytes 691208 | tf_op jit(solution)/shard_map/ppermute | solution.py:24
  50.6 1.6 %collective-permute-start.9 = (bf16[2,40,1440]{2,1,0:T(8,128)(2,1)S(1)}, bf16[2,40,1440]{2,1,0:T(8,128)(2,1)S(1)}, u32[]{:S(2)}, u32[]{:S(2)}) collective-permute-start(bf16[2,40,1440]{2,1,0:T(8,128)(2,1)S(1)} %get-tuple-element.59), channel_id=1, source_target_pairs={{0,4},{2,6},{4,0},{6,2},{8,12},{10,14},{12,8},{14,10},{16,20},{18,... | collective-permute-start | bytes 691208 | tf_op jit(solution)/shard_map/ppermute | solution.py:24
  52.3 6.0 %shard_map.148.refs_0_ = bf16[320,720]{1,0:T(8,128)(2,1)S(1)} custom-call(s32[1]{0:T(128)} %bitcast.me_ref, bf16[3,240,2880]{2,1,0:T(8,128)(2,1)} %bitcast.113, bf16[3,240,2880]{2,1,0:T(8,128)(2,1)} %bitcast.115, f32[1,2880]{1,0:T(1,128)} %reshape.153.gain_ref, bf16[2,160,1440]{2,1,0:T(8,128)(2,1)S(1)} %constant_dynamic-update-slice_fusion.refs_0_, ...), custom_call_target="tpu_custom_call" | custom-call | tf_op jit(solution)/shard_map/pallas_call | solution.py:215
  58.5 3.8 %collective-permute-done.10 = bf16[2,40,1440]{2,1,0:T(8,128)(2,1)S(1)} collective-permute-done((bf16[2,40,1440]{2,1,0:T(8,128)(2,1)S(1)}, bf16[2,40,1440]{2,1,0:T(8,128)(2,1)S(1)}, u32[]{:S(2)}, u32[]{:S(2)}) %collective-permute-start.10) | collective-permute-done | bytes 230432 | tf_op jit(solution)/shard_map/ppermute | solution.py:24
  63.5 1.6 %collective-permute-start.13 = (bf16[320,720]{1,0:T(8,128)(2,1)S(1)}, bf16[320,720]{1,0:T(8,128)(2,1)S(1)}, u32[]{:S(2)}, u32[]{:S(2)}) collective-permute-start(bf16[320,720]{1,0:T(8,128)(2,1)S(1)} %shard_map.148.refs_0_), channel_id=1, source_target_pairs={{0,1},{1,0},{2,3},{3,2},{4,5},{5,4},{6,7},{7,6},{8,9},{9,8},{10,11... | collective-permute-start | bytes 1382408 | tf_op jit(solution)/shard_map/ppermute | solution.py:24
  66.0 6.2 %shard_map.149.refs_0_ = bf16[320,720]{1,0:T(8,128)(2,1)S(1)} custom-call(s32[1]{0:T(128)} %bitcast.me_ref, bf16[3,240,2880]{2,1,0:T(8,128)(2,1)} %bitcast.114, bf16[3,240,2880]{2,1,0:T(8,128)(2,1)} %bitcast.116, f32[1,2880]{1,0:T(1,128)} %reshape.153.gain_ref, bf16[2,160,1440]{2,1,0:T(8,128)(2,1)S(1)} %constant_dynamic-update-slice_fusion.4.refs_0_, ...), custom_call_target="tpu_custom_call" | custom-call | tf_op jit(solution)/shard_map/pallas_call | solution.py:215
  72.2 1.6 %collective-permute-start.18 = (bf16[320,720]{1,0:T(8,128)(2,1)S(1)}, bf16[320,720]{1,0:T(8,128)(2,1)S(1)}, u32[]{:S(2)}, u32[]{:S(2)}) collective-permute-start(bf16[320,720]{1,0:T(8,128)(2,1)S(1)} %shard_map.149.refs_0_), channel_id=1, source_target_pairs={{0,1},{1,0},{2,3},{3,2},{4,5},{5,4},{6,7},{7,6},{8,9},{9,8},{10,11... | collective-permute-start | bytes 1382408 | tf_op jit(solution)/shard_map/ppermute | solution.py:24
  73.8 3.8 %collective-permute-done.13.refs_1_ = bf16[320,720]{1,0:T(8,128)(2,1)S(1)} collective-permute-done((bf16[320,720]{1,0:T(8,128)(2,1)S(1)}, bf16[320,720]{1,0:T(8,128)(2,1)S(1)}, u32[]{:S(2)}, u32[]{:S(2)}) %collective-permute-start.13) | collective-permute-done | bytes 460832 | tf_op jit(solution)/shard_map/ppermute | solution.py:24
  77.6 3.5 %shard_map.150 = (bf16[160,1440]{1,0:T(8,128)(2,1)S(1)}, bf16[160,1440]{1,0:T(8,128)(2,1)S(1)}) custom-call(s32[1]{0:T(128)} %bitcast.me_ref, bf16[2,720,1440]{2,1,0:T(8,128)(2,1)} %bitcast.111, bf16[320,720]{1,0:T(8,128)(2,1)S(1)} %shard_map.148.refs_0_, bf16[320,720]{1,0:T(8,128)(2,1)S(1)} %collective-permute-done.13.refs_1_), custom_call_target="tpu_custom_call" | custom-call | tf_op jit(solution)/shard_map/pallas_call | solution.py:215
  81.4 6.2 %collective-permute-done.18.refs_1_ = bf16[320,720]{1,0:T(8,128)(2,1)S(1)} collective-permute-done((bf16[320,720]{1,0:T(8,128)(2,1)S(1)}, bf16[320,720]{1,0:T(8,128)(2,1)S(1)}, u32[]{:S(2)}, u32[]{:S(2)}) %collective-permute-start.18) | collective-permute-done | bytes 460832 | tf_op jit(solution)/shard_map/ppermute | solution.py:24
  87.6 3.5 %shard_map.151 = (bf16[160,1440]{1,0:T(8,128)(2,1)S(1)}, bf16[160,1440]{1,0:T(8,128)(2,1)S(1)}) custom-call(s32[1]{0:T(128)} %bitcast.me_ref, bf16[2,720,1440]{2,1,0:T(8,128)(2,1)} %bitcast.112, bf16[320,720]{1,0:T(8,128)(2,1)S(1)} %shard_map.149.refs_0_, bf16[320,720]{1,0:T(8,128)(2,1)S(1)} %collective-permute-done.18.refs_1_), custom_call_target="tpu_custom_call" | custom-call | tf_op jit(solution)/shard_map/pallas_call | solution.py:215
  91.4 1.7 %collective-permute-done.19 = bf16[160,1440]{1,0:T(8,128)(2,1)S(1)} collective-permute-done((bf16[160,1440]{1,0:T(8,128)(2,1)S(1)}, bf16[160,1440]{1,0:T(8,128)(2,1)S(1)}, u32[]{:S(2)}, u32[]{:S(2)}) %collective-permute-start.19) | collective-permute-done | bytes 460832 | tf_op jit(solution)/shard_map/ppermute | solution.py:24
  94.3 2.5 %collective-permute-start.22 = (bf16[40,1440]{1,0:T(8,128)(2,1)S(1)}, bf16[40,1440]{1,0:T(8,128)(2,1)S(1)}, u32[]{:S(2)}, u32[]{:S(2)}) collective-permute-start(bf16[40,1440]{1,0:T(8,128)(2,1)S(1)} %get-tuple-element.66), channel_id=1, source_target_pairs={{0,12},{2,14},{4,8},{6,10},{8,4},{10,6},{12,0},{14,2},{16,28},{18,... | collective-permute-start | bytes 345608 | tf_op jit(solution)/shard_map/ppermute | solution.py:24
  98.7 1.7 %collective-permute-start.17 = (bf16[40,1440]{1,0:T(8,128)(2,1)S(1)}, bf16[40,1440]{1,0:T(8,128)(2,1)S(1)}, u32[]{:S(2)}, u32[]{:S(2)}) collective-permute-start(bf16[40,1440]{1,0:T(8,128)(2,1)S(1)} %get-tuple-element.70), channel_id=1, source_target_pairs={{0,12},{2,14},{4,8},{6,10},{8,4},{10,6},{12,0},{14,2},{16,28},{18,... | collective-permute-start | bytes 345608 | tf_op jit(solution)/shard_map/ppermute | solution.py:24
  100.4 3.2 %collective-permute-done.22 = bf16[40,1440]{1,0:T(8,128)(2,1)S(1)} collective-permute-done((bf16[40,1440]{1,0:T(8,128)(2,1)S(1)}, bf16[40,1440]{1,0:T(8,128)(2,1)S(1)}, u32[]{:S(2)}, u32[]{:S(2)}) %collective-permute-start.22) | collective-permute-done | bytes 115232 | tf_op jit(solution)/shard_map/ppermute | solution.py:24
  104.1 1.9 %collective-permute-start.23 = (bf16[64,1440]{1,0:T(8,128)(2,1)S(1)}, bf16[64,1440]{1,0:T(8,128)(2,1)S(1)}, u32[]{:S(2)}, u32[]{:S(2)}) collective-permute-start(bf16[64,1440]{1,0:T(8,128)(2,1)S(1)} %fusion.3), channel_id=1, source_target_pairs={{0,16},{2,18},{4,20},{6,22},{8,24},{10,26},{12,28},{14,30},{16,0},... | collective-permute-start | bytes 552968 | tf_op jit(solution)/shard_map/ppermute | solution.py:24
  106.0 4.7 %collective-permute-done.17 = bf16[40,1440]{1,0:T(8,128)(2,1)S(1)} collective-permute-done((bf16[40,1440]{1,0:T(8,128)(2,1)S(1)}, bf16[40,1440]{1,0:T(8,128)(2,1)S(1)}, u32[]{:S(2)}, u32[]{:S(2)}) %collective-permute-start.17) | collective-permute-done | bytes 115232 | tf_op jit(solution)/shard_map/ppermute | solution.py:24
  110.9 3.4 %collective-permute-done.23 = bf16[64,1440]{1,0:T(8,128)(2,1)S(1)} collective-permute-done((bf16[64,1440]{1,0:T(8,128)(2,1)S(1)}, bf16[64,1440]{1,0:T(8,128)(2,1)S(1)}, u32[]{:S(2)}, u32[]{:S(2)}) %collective-permute-start.23) | collective-permute-done | bytes 184352 | tf_op jit(solution)/shard_map/ppermute | solution.py:24
  (80 shorter events, 17.4 us)
Async XLA Ops:
  0.0 20.2 %copy-start.1 = (f32[2880]{0:T(1024)S(1)}, f32[2880]{0:T(1024)}, u32[]{:S(2)}) copy-start(f32[2880]{0:T(1024)} %param.24) | copy-start | bytes 34564
  0.0 15.5 %all-to-all-start = ((bf16[16,8,512]{2,1,0:T(8,128)(2,1)}), bf16[16,8,512]{2,1,0:T(8,128)(2,1)S(1)}, u32[]{:S(2)}, u32[]{:S(2)}) async-start(bf16[16,8,512]{2,1,0:T(8,128)(2,1)} %bitcast.121), calls=%async_computation | async-start | bytes 262144 | tf_op jit(solution)/shard_map/all_to_all | solution.py:256
  9.4 0.7 copy-start
  18.4 5.3 %copy-start.2 = (f32[64,4]{0,1:T(4,128)S(1)}, f32[64,4]{0,1:T(4,128)}, u32[]{:S(2)}) copy-start(f32[64,4]{0,1:T(4,128)} %param.26) | copy-start | bytes 3076
  18.4 6.2 %collective-permute-start = (bf16[64,1440]{1,0:T(8,128)(2,1)S(1)}, bf16[64,1440]{1,0:T(8,128)(2,1)S(1)}, u32[]{:S(2)}, u32[]{:S(2)}) collective-permute-start(bf16[64,1440]{1,0:T(8,128)(2,1)S(1)} %get-tuple-element.37), channel_id=1, source_target_pairs={{0,1},{1,0},{2,3},{3,2},{4,5},{5,4},{6,7},{7,6},{8,9},{9,8},{10,11... | collective-permute-start | bytes 552968 | tf_op jit(solution)/shard_map/ppermute | solution.py:24
  24.6 12.7 %collective-permute-start.4 = (bf16[64,1440]{1,0:T(8,128)(2,1)S(1)}, bf16[64,1440]{1,0:T(8,128)(2,1)S(1)}, u32[]{:S(2)}, u32[]{:S(2)}) collective-permute-start(bf16[64,1440]{1,0:T(8,128)(2,1)S(1)} %fusion.4), channel_id=1, source_target_pairs={{0,16},{2,18},{4,20},{6,22},{8,24},{10,26},{12,28},{14,30},{16,0},... | collective-permute-start | bytes 552968 | tf_op jit(solution)/shard_map/ppermute | solution.py:24
  27.1 5.8 %collective-permute-start.1 = (bf16[64,1440]{1,0:T(8,128)(2,1)S(1)}, bf16[64,1440]{1,0:T(8,128)(2,1)S(1)}, u32[]{:S(2)}, u32[]{:S(2)}) collective-permute-start(bf16[64,1440]{1,0:T(8,128)(2,1)S(1)} %get-tuple-element.40), channel_id=1, source_target_pairs={{0,1},{1,0},{2,3},{3,2},{4,5},{5,4},{6,7},{7,6},{8,9},{9,8},{10,11... | collective-permute-start | bytes 552968 | tf_op jit(solution)/shard_map/ppermute | solution.py:24
  33.4 9.0 %collective-permute-start.3 = (bf16[2,40,1440]{2,1,0:T(8,128)(2,1)S(1)}, bf16[2,40,1440]{2,1,0:T(8,128)(2,1)S(1)}, u32[]{:S(2)}, u32[]{:S(2)}) collective-permute-start(bf16[2,40,1440]{2,1,0:T(8,128)(2,1)S(1)} %get-tuple-element.63), channel_id=1, source_target_pairs={{0,8},{2,10},{4,12},{6,14},{8,0},{10,2},{12,4},{14,6},{16,24},{18,... | collective-permute-start | bytes 691208 | tf_op jit(solution)/shard_map/ppermute | solution.py:24
  34.9 6.2 %collective-permute-start.2 = (f32[64,8]{0,1:T(8,128)S(1)}, f32[64,8]{0,1:T(8,128)S(1)}, u32[]{:S(2)}, u32[]{:S(2)}) collective-permute-start(f32[64,8]{0,1:T(8,128)S(1)} %pad_maximum_fusion.8), channel_id=1, source_target_pairs={{0,16},{2,18},{4,20},{6,22},{8,24},{10,26},{12,28},{14,30},{16,0},... | collective-permute-start | bytes 6152 | tf_op jit(solution)/shard_map/ppermute | solution.py:24
  35.5 12.1 %collective-permute-start.7 = (bf16[2,40,1440]{2,1,0:T(8,128)(2,1)S(1)}, bf16[2,40,1440]{2,1,0:T(8,128)(2,1)S(1)}, u32[]{:S(2)}, u32[]{:S(2)}) collective-permute-start(bf16[2,40,1440]{2,1,0:T(8,128)(2,1)S(1)} %get-tuple-element.61), channel_id=1, source_target_pairs={{0,12},{2,14},{4,8},{6,10},{8,4},{10,6},{12,0},{14,2},{16,28},{18,... | collective-permute-start | bytes 691208 | tf_op jit(solution)/shard_map/ppermute | solution.py:24
  37.0 11.5 %collective-permute-start.6 = (bf16[2,40,1440]{2,1,0:T(8,128)(2,1)S(1)}, bf16[2,40,1440]{2,1,0:T(8,128)(2,1)S(1)}, u32[]{:S(2)}, u32[]{:S(2)}) collective-permute-start(bf16[2,40,1440]{2,1,0:T(8,128)(2,1)S(1)} %get-tuple-element.64), channel_id=1, source_target_pairs={{0,4},{2,6},{4,0},{6,2},{8,12},{10,14},{12,8},{14,10},{16,20},{18,... | collective-permute-start | bytes 691208 | tf_op jit(solution)/shard_map/ppermute | solution.py:24
  37.4 5.7 %collective-permute-start.5 = (bf16[64,1440]{1,0:T(8,128)(2,1)S(1)}, bf16[64,1440]{1,0:T(8,128)(2,1)S(1)}, u32[]{:S(2)}, u32[]{:S(2)}) collective-permute-start(bf16[64,1440]{1,0:T(8,128)(2,1)S(1)} %collective-permute-done.4), channel_id=1, source_target_pairs={{0,1},{1,0},{2,3},{3,2},{4,5},{5,4},{6,7},{7,6},{8,9},{9,8},{10,11... | collective-permute-start | bytes 552968 | tf_op jit(solution)/shard_map/ppermute | solution.py:24
  48.5 3.7 %collective-permute-start.8 = (bf16[2,160,1440]{2,1,0:T(8,128)(2,1)S(1)}, bf16[2,160,1440]{2,1,0:T(8,128)(2,1)S(1)}, u32[]{:S(2)}, u32[]{:S(2)}) collective-permute-start(bf16[2,160,1440]{2,1,0:T(8,128)(2,1)S(1)} %constant_dynamic-update-slice_fusion.refs_0_), channel_id=1, source_target_pairs={{0,2},{2,0},{4,6},{6,4},{8,10},{10,8},{12,14},{14,12},{16,18},{18,... | collective-permute-start | bytes 2764808 | tf_op jit(solution)/shard_map/ppermute | solution.py:24
  48.7 9.8 %collective-permute-start.11 = (bf16[2,40,1440]{2,1,0:T(8,128)(2,1)S(1)}, bf16[2,40,1440]{2,1,0:T(8,128)(2,1)S(1)}, u32[]{:S(2)}, u32[]{:S(2)}) collective-permute-start(bf16[2,40,1440]{2,1,0:T(8,128)(2,1)S(1)} %get-tuple-element.57), channel_id=1, source_target_pairs={{0,12},{2,14},{4,8},{6,10},{8,4},{10,6},{12,0},{14,2},{16,28},{18,... | collective-permute-start | bytes 691208 | tf_op jit(solution)/shard_map/ppermute | solution.py:24
  49.2 13.1 %collective-permute-start.10 = (bf16[2,40,1440]{2,1,0:T(8,128)(2,1)S(1)}, bf16[2,40,1440]{2,1,0:T(8,128)(2,1)S(1)}, u32[]{:S(2)}, u32[]{:S(2)}) collective-permute-start(bf16[2,40,1440]{2,1,0:T(8,128)(2,1)S(1)} %get-tuple-element.60), channel_id=1, source_target_pairs={{0,8},{2,10},{4,12},{6,14},{8,0},{10,2},{12,4},{14,6},{16,24},{18,... | collective-permute-start | bytes 691208 | tf_op jit(solution)/shard_map/ppermute | solution.py:24
  50.6 12.7 %collective-permute-start.9 = (bf16[2,40,1440]{2,1,0:T(8,128)(2,1)S(1)}, bf16[2,40,1440]{2,1,0:T(8,128)(2,1)S(1)}, u32[]{:S(2)}, u32[]{:S(2)}) collective-permute-start(bf16[2,40,1440]{2,1,0:T(8,128)(2,1)S(1)} %get-tuple-element.59), channel_id=1, source_target_pairs={{0,4},{2,6},{4,0},{6,2},{8,12},{10,14},{12,8},{14,10},{16,20},{18,... | collective-permute-start | bytes 691208 | tf_op jit(solution)/shard_map/ppermute | solution.py:24
  63.4 2.6 %collective-permute-start.12 = (bf16[2,160,1440]{2,1,0:T(8,128)(2,1)S(1)}, bf16[2,160,1440]{2,1,0:T(8,128)(2,1)S(1)}, u32[]{:S(2)}, u32[]{:S(2)}) collective-permute-start(bf16[2,160,1440]{2,1,0:T(8,128)(2,1)S(1)} %constant_dynamic-update-slice_fusion.4.refs_0_), channel_id=1, source_target_pairs={{0,2},{2,0},{4,6},{6,4},{8,10},{10,8},{12,14},{14,12},{16,18},{18,... | collective-permute-start | bytes 2764808 | tf_op jit(solution)/shard_map/ppermute | solution.py:24
  63.5 14.1 %collective-permute-start.13 = (bf16[320,720]{1,0:T(8,128)(2,1)S(1)}, bf16[320,720]{1,0:T(8,128)(2,1)S(1)}, u32[]{:S(2)}, u32[]{:S(2)}) collective-permute-start(bf16[320,720]{1,0:T(8,128)(2,1)S(1)} %shard_map.148.refs_0_), channel_id=1, source_target_pairs={{0,1},{1,0},{2,3},{3,2},{4,5},{5,4},{6,7},{7,6},{8,9},{9,8},{10,11... | collective-permute-start | bytes 1382408 | tf_op jit(solution)/shard_map/ppermute | solution.py:24
  72.2 15.4 %collective-permute-start.18 = (bf16[320,720]{1,0:T(8,128)(2,1)S(1)}, bf16[320,720]{1,0:T(8,128)(2,1)S(1)}, u32[]{:S(2)}, u32[]{:S(2)}) collective-permute-start(bf16[320,720]{1,0:T(8,128)(2,1)S(1)} %shard_map.149.refs_0_), channel_id=1, source_target_pairs={{0,1},{1,0},{2,3},{3,2},{4,5},{5,4},{6,7},{7,6},{8,9},{9,8},{10,11... | collective-permute-start | bytes 1382408 | tf_op jit(solution)/shard_map/ppermute | solution.py:24
  81.1 10.2 %collective-permute-start.14 = (bf16[160,1440]{1,0:T(8,128)(2,1)S(1)}, bf16[160,1440]{1,0:T(8,128)(2,1)S(1)}, u32[]{:S(2)}, u32[]{:S(2)}) collective-permute-start(bf16[160,1440]{1,0:T(8,128)(2,1)S(1)} %get-tuple-element.53), channel_id=1, source_target_pairs={{0,2},{2,0},{4,6},{6,4},{8,10},{10,8},{12,14},{14,12},{16,18},{18,... | collective-permute-start | bytes 1382408 | tf_op jit(solution)/shard_map/ppermute | solution.py:24
  91.2 1.9 %collective-permute-start.19 = (bf16[160,1440]{1,0:T(8,128)(2,1)S(1)}, bf16[160,1440]{1,0:T(8,128)(2,1)S(1)}, u32[]{:S(2)}, u32[]{:S(2)}) collective-permute-start(bf16[160,1440]{1,0:T(8,128)(2,1)S(1)} %get-tuple-element.56), channel_id=1, source_target_pairs={{0,2},{2,0},{4,6},{6,4},{8,10},{10,8},{12,14},{14,12},{16,18},{18,... | collective-permute-start | bytes 1382408 | tf_op jit(solution)/shard_map/ppermute | solution.py:24
  93.2 5.4 %collective-permute-start.20 = (bf16[40,1440]{1,0:T(8,128)(2,1)S(1)}, bf16[40,1440]{1,0:T(8,128)(2,1)S(1)}, u32[]{:S(2)}, u32[]{:S(2)}) collective-permute-start(bf16[40,1440]{1,0:T(8,128)(2,1)S(1)} %get-tuple-element.68), channel_id=1, source_target_pairs={{0,4},{2,6},{4,0},{6,2},{8,12},{10,14},{12,8},{14,10},{16,20},{18,... | collective-permute-start | bytes 345608 | tf_op jit(solution)/shard_map/ppermute | solution.py:24
  93.9 6.5 %collective-permute-start.21 = (bf16[40,1440]{1,0:T(8,128)(2,1)S(1)}, bf16[40,1440]{1,0:T(8,128)(2,1)S(1)}, u32[]{:S(2)}, u32[]{:S(2)}) collective-permute-start(bf16[40,1440]{1,0:T(8,128)(2,1)S(1)} %get-tuple-element.67), channel_id=1, source_target_pairs={{0,8},{2,10},{4,12},{6,14},{8,0},{10,2},{12,4},{14,6},{16,24},{18,... | collective-permute-start | bytes 345608 | tf_op jit(solution)/shard_map/ppermute | solution.py:24
  94.3 9.3 %collective-permute-start.22 = (bf16[40,1440]{1,0:T(8,128)(2,1)S(1)}, bf16[40,1440]{1,0:T(8,128)(2,1)S(1)}, u32[]{:S(2)}, u32[]{:S(2)}) collective-permute-start(bf16[40,1440]{1,0:T(8,128)(2,1)S(1)} %get-tuple-element.66), channel_id=1, source_target_pairs={{0,12},{2,14},{4,8},{6,10},{8,4},{10,6},{12,0},{14,2},{16,28},{18,... | collective-permute-start | bytes 345608 | tf_op jit(solution)/shard_map/ppermute | solution.py:24
  96.8 9.2 %collective-permute-start.15 = (bf16[40,1440]{1,0:T(8,128)(2,1)S(1)}, bf16[40,1440]{1,0:T(8,128)(2,1)S(1)}, u32[]{:S(2)}, u32[]{:S(2)}) collective-permute-start(bf16[40,1440]{1,0:T(8,128)(2,1)S(1)} %get-tuple-element.72), channel_id=1, source_target_pairs={{0,4},{2,6},{4,0},{6,2},{8,12},{10,14},{12,8},{14,10},{16,20},{18,... | collective-permute-start | bytes 345608 | tf_op jit(solution)/shard_map/ppermute | solution.py:24
  97.5 8.5 %collective-permute-start.16 = (bf16[40,1440]{1,0:T(8,128)(2,1)S(1)}, bf16[40,1440]{1,0:T(8,128)(2,1)S(1)}, u32[]{:S(2)}, u32[]{:S(2)}) collective-permute-start(bf16[40,1440]{1,0:T(8,128)(2,1)S(1)} %get-tuple-element.71), channel_id=1, source_target_pairs={{0,8},{2,10},{4,12},{6,14},{8,0},{10,2},{12,4},{14,6},{16,24},{18,... | collective-permute-start | bytes 345608 | tf_op jit(solution)/shard_map/ppermute | solution.py:24
  98.7 12.0 %collective-permute-start.17 = (bf16[40,1440]{1,0:T(8,128)(2,1)S(1)}, bf16[40,1440]{1,0:T(8,128)(2,1)S(1)}, u32[]{:S(2)}, u32[]{:S(2)}) collective-permute-start(bf16[40,1440]{1,0:T(8,128)(2,1)S(1)} %get-tuple-element.70), channel_id=1, source_target_pairs={{0,12},{2,14},{4,8},{6,10},{8,4},{10,6},{12,0},{14,2},{16,28},{18,... | collective-permute-start | bytes 345608 | tf_op jit(solution)/shard_map/ppermute | solution.py:24
  104.1 10.2 %collective-permute-start.23 = (bf16[64,1440]{1,0:T(8,128)(2,1)S(1)}, bf16[64,1440]{1,0:T(8,128)(2,1)S(1)}, u32[]{:S(2)}, u32[]{:S(2)}) collective-permute-start(bf16[64,1440]{1,0:T(8,128)(2,1)S(1)} %fusion.3), channel_id=1, source_target_pairs={{0,16},{2,18},{4,20},{6,22},{8,24},{10,26},{12,28},{14,30},{16,0},... | collective-permute-start | bytes 552968 | tf_op jit(solution)/shard_map/ppermute | solution.py:24
